TPU v7x, 32 devices: a whole 2x2x4 slice. The times are simulated.
32 devices in a mesh: grp: 4 (over x, core), dev: 8 (over z, y).
Axes of the slice: x: 2, y: 2, z: 4, core: 2. Of those that a mesh axis runs over, the one named last changes fastest.
Arguments:
- ref_pos: float32 [3, 262144], P(None, ('grp', 'dev')), may hold values from -4 to 4
- displacement: float32 [3, 262144], P(None, ('grp', 'dev')), may hold values from -0.6 to 0.6
- velocity: float32 [3, 262144], P(None, ('grp', 'dev')), may hold values from -6 to 6
- node_mass: float32 [262144], P(('grp', 'dev')), may hold values from 0.5 to 2
- elem_nodes: int32 [4, 262144], P(None, ('grp', 'dev')), may hold values from 0 to 8191
- elem_part: int32 [262144], P(('grp', 'dev')), may hold values from 0 to 127, as said below
- elem_scale: float32 [262144], P(('grp', 'dev')), may hold values from 0.5 to 2
- part_stiff: float32 [128], P(('grp', 'dev')), may hold values from 1 to 100
- shared: int32 [2, 65536], P(None, ('grp', 'dev')), may hold values from 0 to 8191, as said below
- seg_node: int32 [2048, 128], P(('grp', 'dev')), may hold values from 0 to 8191
- seg_mask: int32 [2048, 128], P(('grp', 'dev')), may hold values 0 or 1
- send_blk: int32 [32, 32, 5], P(('grp', 'dev')), may hold values from 0 to 63
- pair_a: int32 [16384], P(('grp', 'dev')), may hold values from 0 to 63
- pair_slot: int32 [16384], P(('grp', 'dev')), may hold values from 0 to 159
- pair_mask: int32 [16384], P(('grp', 'dev')), may hold values from 0 to 1, as said below
Outputs:
- new_displace: float32 [3, 262144], P(None, ('grp', 'dev'))
- new_velocity: float32 [3, 262144], P(None, ('grp', 'dev'))
Inputs may be any that keep to these rules, and one draw needn't show every extreme that they name: `elem_part`: the elements of device d belong to parts d * 4 to (d + 1) * 4 - 1. `shared`: the 4096 entries of one device are different nodes; row 1 of device k and row 0 of device k + 1 of the same group name the same physical nodes, entry by entry. `pair_mask`: in each device's 512 pair slots the live ones come first; each device has 128 or more live, and some device has all 512 live.
All inputs are finite; a program needn't handle non-finite values. No bound on the sum of `seg_mask` on one device may be relied on, other than what follows from the above.
Results may differ from a plain program's by a relative error of at most 0.000062.
Values sent between devices are 32-bit elements; how exact they have to be, the bound alone decides.
A program may use at most 128 MiB of HBM per device.

v0:
```python
import math

import jax
import jax.numpy as jnp
from jax import lax
from jax.sharding import PartitionSpec as P

SPRINGS = ((0, 1, 1.0), (1, 2, 1.0), (2, 3, 1.0), (3, 0, 1.0), (0, 2, 0.5), (1, 3, 0.5))
COURANT = 0.5
EXACT = lax.Precision.HIGHEST


def shifted(value, axis, steps):
    count = lax.axis_size(axis)
    first, last = (max(0, -steps), min(count, count - steps))
    return lax.ppermute(value, axis, [(source, source + steps) for source in range(first, last)])


def one_hot_rows(index_list, count):
    return (jnp.arange(count, dtype=jnp.int32)[:, None] == index_list[None, :]).astype(jnp.float32)


def pick_dot(selector, table):
    return jnp.dot(selector, table, precision=EXACT, preferred_element_type=jnp.float32)


def corner_forces(corner, elem_stiff):
    corner_force = [jnp.zeros_like(corner[:, 0]) for corner_index in range(4)]
    for head_node, tail_node, weight in SPRINGS:
        pull_term = weight * elem_stiff * (corner[:, tail_node] - corner[:, head_node])
        corner_force[head_node] = corner_force[head_node] + pull_term
        corner_force[tail_node] = corner_force[tail_node] - pull_term
    return jnp.stack(corner_force, 1)


def pair_forces(near_pos, far_pos, near_mask, far_mask, live_pair):
    offset = near_pos[:, :, :, None] - far_pos[:, :, None, :]
    weights = jnp.exp(-jnp.sum(offset * offset, 1))
    weights = weights * (near_mask[:, :, None] * far_mask[:, None, :]) * live_pair[:, None, None]
    pushed = jnp.sum(weights[:, None] * offset, 3)
    recoil = -jnp.sum(weights[:, None] * offset, 2)
    return (pushed, recoil)


def contact_sums(own_blocks, own_mask, recv_blocks, recv_mask, pair_first, pair_second, pair_live):
    pair_count = pair_first.shape[0]
    group_width = math.gcd(pair_count, 32)
    seg_width = own_blocks.shape[2]
    own_count = own_blocks.shape[0]
    recv_count = recv_blocks.shape[0]
    own_table = jnp.concatenate([own_blocks.reshape(own_count, 3 * seg_width), own_mask], 1)
    recv_table = jnp.concatenate([recv_blocks.reshape(recv_count, 3 * seg_width), recv_mask], 1)

    def one_group(group_index):
        group_start = group_index * group_width
        first_ids = lax.dynamic_slice_in_dim(pair_first, group_start, group_width)
        second_ids = lax.dynamic_slice_in_dim(pair_second, group_start, group_width)
        live_part = lax.dynamic_slice_in_dim(pair_live, group_start, group_width)
        near_rows = pick_dot(one_hot_rows(first_ids, own_count).T, own_table)
        far_rows = pick_dot(one_hot_rows(second_ids, recv_count).T, recv_table)
        near_pos = near_rows[:, : 3 * seg_width].reshape(group_width, 3, seg_width)
        far_pos = far_rows[:, : 3 * seg_width].reshape(group_width, 3, seg_width)
        return pair_forces(
            near_pos,
            far_pos,
            near_rows[:, 3 * seg_width :],
            far_rows[:, 3 * seg_width :],
            live_part,
        )

    pushed, recoil = lax.map(one_group, jnp.arange(pair_count // group_width, dtype=jnp.int32))
    pushed = pushed.reshape(pair_count, 3 * seg_width)
    recoil = recoil.reshape(pair_count, 3 * seg_width)
    own_force = pick_dot(one_hot_rows(pair_first, own_count), pushed).reshape(
        own_count, 3, seg_width
    )
    far_force = pick_dot(one_hot_rows(pair_second, recv_count), recoil).reshape(
        recv_count, 3, seg_width
    )
    return (own_force, far_force)


def shards(
    ref_pos,
    displacement,
    velocity,
    node_mass,
    elem_nodes,
    elem_part,
    elem_scale,
    part_stiff,
    shared,
    seg_node,
    seg_mask,
    send_blk,
    pair_a,
    pair_slot,
    pair_mask,
):
    groups = lax.axis_size("grp")
    within = lax.axis_size("dev")
    devices = groups * within
    part_count = part_stiff.shape[0]
    local_part = elem_part - lax.axis_index(("grp", "dev")) * part_count
    chooser = local_part[None, :] == jnp.arange(part_count, dtype=jnp.int32)[:, None]
    elem_stiff = jnp.sum(jnp.where(chooser, part_stiff[:, None], 0.0), 0) * elem_scale
    elem_count = elem_nodes.shape[1]
    block_count = seg_node.shape[0]
    seg_width = seg_node.shape[1]
    node_rows = jnp.concatenate([displacement, node_mass[None, :], ref_pos], 0)
    all_index = jnp.concatenate([elem_nodes.reshape(-1), seg_node.reshape(-1)], 0)
    picked = node_rows[:, all_index]
    corner = picked[0:3, : 4 * elem_count].reshape(3, 4, elem_count)
    elem_mass = jnp.min(picked[3, : 4 * elem_count].reshape(4, elem_count), 0)
    stacked = corner_forces(corner, elem_stiff)
    step_limit = jnp.min(COURANT * jnp.sqrt(elem_mass / elem_stiff))
    seg_rows = picked[:, 4 * elem_count :]
    position = (seg_rows[0:3] + seg_rows[4:7]).reshape(3, block_count, seg_width)
    blocks = jnp.moveaxis(position, 1, 0)
    seg_weight = seg_mask.astype(jnp.float32)
    chosen = send_blk[0]
    outgoing = blocks[chosen]
    out_mask = seg_weight[chosen]
    cap_count = chosen.shape[1]
    stamp = jnp.full((devices, 1), step_limit, jnp.float32)
    arrived, arrived_mask, stamps = (
        lax.all_to_all(outgoing, ("grp", "dev"), split_axis=0, concat_axis=0, tiled=True),
        lax.all_to_all(out_mask, ("grp", "dev"), split_axis=0, concat_axis=0, tiled=True),
        lax.all_to_all(stamp, ("grp", "dev"), split_axis=0, concat_axis=0, tiled=True),
    )
    time_step = jnp.min(stamps)
    own_force, far_force = contact_sums(
        blocks,
        seg_weight,
        arrived.reshape(devices * cap_count, 3, seg_width),
        arrived_mask.reshape(devices * cap_count, seg_width),
        pair_a,
        pair_slot,
        pair_mask.astype(jnp.float32),
    )
    far_grid = far_force.reshape(devices, cap_count, 3, seg_width)
    returned = lax.all_to_all(far_grid, ("grp", "dev"), split_axis=0, concat_axis=0, tiled=True)
    back_force = pick_dot(
        one_hot_rows(chosen.reshape(-1), block_count),
        returned.reshape(devices * cap_count, 3 * seg_width),
    )
    seg_force = own_force + back_force.reshape(block_count, 3, seg_width)
    flat_force = jnp.moveaxis(seg_force, 1, 0).reshape(3, -1)
    all_force = jnp.concatenate([stacked.reshape(3, -1), flat_force], 1)
    totals = jnp.zeros_like(displacement).at[:, all_index].add(all_force)
    share_count = shared.shape[1]
    share_flat = shared.reshape(-1)
    share_rows = totals[:, share_flat]
    upper_rows = share_rows[:, :share_count]
    lower_rows = share_rows[:, share_count:]
    from_lower = shifted(lower_rows, "dev", 1)
    from_upper = shifted(upper_rows, "dev", -1)
    assembled = totals.at[:, share_flat].add(jnp.concatenate([from_lower, from_upper], 1))
    accelerate = assembled / node_mass[None, :]
    new_velocity = velocity + time_step * accelerate
    new_displace = displacement + time_step * new_velocity
    return (new_displace, new_velocity)


def solution(mesh):
    return jax.shard_map(
        shards,
        mesh=mesh,
        in_specs=(
            P(None, ("grp", "dev")),
            P(None, ("grp", "dev")),
            P(None, ("grp", "dev")),
            P(("grp", "dev")),
            P(None, ("grp", "dev")),
            P(("grp", "dev")),
            P(("grp", "dev")),
            P(("grp", "dev")),
            P(None, ("grp", "dev")),
            P(("grp", "dev"), None),
            P(("grp", "dev"), None),
            P(("grp", "dev"), None, None),
            P(("grp", "dev")),
            P(("grp", "dev")),
            P(("grp", "dev")),
        ),
        out_specs=(P(None, ("grp", "dev")), P(None, ("grp", "dev"))),
        check_vma=False,
    )
```

profile of v0, /device:TPU:0, one launch (start us, length us, event | category | flops | bytes accessed | tf_op | source)
XLA Modules:
  0.0 691.8 jit_solution(17496700260357090692)
XLA Ops:
  3.7 7.3 %all-to-all-start.2 = ((f32[32,5,128]{2,1,0:T(8,128)}), f32[32,5,128]{2,1,0:T(8,128)S(1)}, u32[]{:S(2)}, u32[]{:S(2)}) async-start(f32[32,5,128]{2,1,0:T(8,128)} %reshape.314), calls=%async_computation.2 | async-start | bytes 262144 | tf_op jit(solution)/shard_map/all_to_all | solution.py:128
  11.0 1.1 pad_maximum_fusion.1
  12.1 2.7 copy.119
  15.8 138.0 %gather_fusion = f32[40960,7]{1,0:T(8,128)} fusion(f32[7,8192]{0,1:T(8,128)} %copy.119, s32[40960]{0:T(1024)S(1)} %broadcast_clamp_fusion), kind=kCustom, calls=%fused_computation | custom fusion | bytes 2457600 | tf_op jit(solution)/shard_map/gather | solution.py:112
  153.8 12.7 %slice_reduce_fusion = f32[32768]{0:T(1024)S(1)} fusion(f32[7,40960]{0,1:T(8,128)} %bitcast.106), kind=kLoop, calls=%fused_computation.20 | loop fusion | bytes 262144 | tf_op jit(solution)/shard_map/slice | solution.py:114
  166.5 6.6 slice_add_fusion
  173.1 6.0 slice.76
  179.2 12.3 %fusion.24 = (f32[3,1,8192]{0,2,1:T(8,128)}, f32[3,1,8192]{0,2,1:T(8,128)}, f32[3,1,8192]{0,2,1:T(8,128)}, f32[3,1,8192]{0,2,1:T(8,128)}) fusion(f32[3,4,8192]{0,2,1:T(8,128)} %bitcast.109), kind=kLoop, calls=%fused_computation.76 | loop fusion | bytes 786432 | tf_op jit(solution)/shard_map/slice | solution.py:30
  191.4 2.8 copy.139
  194.3 2.9 copy.140
  197.2 2.9 copy.141
  200.0 2.9 copy.142
  204.5 2.8 copy.125
  207.3 1.5 gather_fusion.1
  208.9 6.0 all-to-all-start.1
  215.4 11.4 %all-to-all-done.1 = f32[32,5,3,128]{3,2,1,0:T(4,128)S(1)} async-done(((f32[32,5,3,128]{3,2,1,0:T(4,128)}), f32[32,5,3,128]{3,2,1,0:T(4,128)S(1)}, u32[]{:S(2)}, u32[]{:S(2)}) %all-to-all-start.1) | async-done | bytes 245792 | tf_op jit(solution)/shard_map/all_to_all | solution.py:127
  226.9 152.4 %while.12 = (s32[]{:T(128)}, f32[16,32,3,128]{3,2,1,0:T(4,128)S(1)}, f32[16,32,3,128]{3,2,1,0:T(4,128)S(1)}, s32[16]{0:T(128)S(1)}, s32[512]{0:T(512)}, /*index=...) while((s32[]{:T(128)}, ...), condition=%wide.region_8.9_spmd, body=%wide.region_4.8_spmd.sunk | while | flops 56617988 | bytes 10028367 | solution.py:71
  229.5 2.1 fusion.40
  232.4 4.0 fusion.41
  239.0 2.1 fusion.40
  241.9 4.0 fusion.41
  248.5 2.1 fusion.40
  251.4 4.0 fusion.41
  258.0 2.1 fusion.40
  261.0 4.0 fusion.41
  267.6 2.1 fusion.40
  270.5 4.0 fusion.41
  277.1 2.1 fusion.40
  280.0 4.0 fusion.41
  286.6 2.1 fusion.40
  289.5 4.0 fusion.41
  296.2 2.1 fusion.40
  299.1 4.0 fusion.41
  305.7 2.1 fusion.40
  308.6 4.0 fusion.41
  315.2 2.1 fusion.40
  318.1 4.0 fusion.41
  324.7 2.1 fusion.40
  327.6 4.0 fusion.41
  334.3 2.1 fusion.40
  337.2 4.0 fusion.41
  343.8 2.1 fusion.40
  346.7 4.0 fusion.41
  353.3 2.1 fusion.40
  356.2 4.0 fusion.41
  362.8 2.1 fusion.40
  365.7 4.0 fusion.41
  372.4 2.1 fusion.40
  375.3 4.0 fusion.41
  380.3 0.9 copy.130
  381.2 3.3 all-to-all-start.3
  386.0 1.2 fusion.18
  387.2 9.5 %all-to-all-done.3 = f32[32,5,3,128]{3,2,1,0:T(4,128)} async-done(((f32[32,5,3,128]{3,2,1,0:T(4,128)}), f32[32,5,3,128]{3,2,1,0:T(4,128)}, u32[]{:S(2)}, u32[]{:S(2)}) %all-to-all-start.3) | async-done | bytes 245792 | tf_op jit(solution)/shard_map/all_to_all | solution.py:142
  396.6 1.2 fusion.9
  398.1 10.0 %copy.132 = f32[40960,3]{1,0:T(8,128)} copy(f32[40960,3]{0,1:T(4,128)S(1)} %maximum_bitcast_fusion) | data formatting | bytes 983040 | tf_op jit(solution)/shard_map/concatenate | solution.py:149
  408.1 219.6 %scatter_custom_fusion = f32[3,8192]{0,1:T(8,128)} fusion(s32[40960]{0:T(1024)} %bitcast.124, f32[40960,3]{1,0:T(8,128)} %copy.132, f32[]{:T(128)} %constant.13.clone.1), kind=kCustom, calls=%fused_computation.22 | custom fusion | flops 122880 | bytes 98816 | tf_op jit(solution)/shard_map/scatter-add | solution.py:150
  627.7 16.3 %gather_fusion.3 = f32[4096,3]{1,0:T(8,128)} fusion(f32[3,8192]{0,1:T(8,128)} %scatter_custom_fusion, s32[4096]{0:T(1024)S(1)} %broadcast_clamp_fusion.1), kind=kCustom, calls=%fused_computation.3 | custom fusion | bytes 114688 | tf_op jit(solution)/shard_map/gather | solution.py:153
  644.1 1.7 fusion.25
  646.1 1.3 collective-permute-start.1
  647.7 4.5 collective-permute-start
  653.0 9.1 %all_to_all.21 = f32[32,1,1]{2,1,0:T(1,128)S(1)} all-to-all(f32[32,1,1]{2,1,0:T(1,128)S(1)} %broadcast_in_dim.23), channel_id=1, replica_groups=mesh['grp'=4,'dev'=8] {'grp','dev'}, dimensions={0} | all-to-all | bytes 256 | tf_op jit(solution)/shard_map/all_to_all | solution.py:129
  663.4 24.2 %scatter_fusion = f32[3,8192]{0,1:T(8,128)} fusion(f32[3,8192]{0,1:T(8,128)} %scatter_custom_fusion, s32[4096]{0:T(1024)S(1)} %bitcast.129, f32[4096,3]{1,0:T(8,128)S(1)} %copy.135), kind=kCustom, calls=%fused_computation.5 | custom fusion | flops 12288 | bytes 163840 | tf_op jit(solution)/shard_map/scatter-add | solution.py:158
  687.6 2.8 copy.136
  690.5 1.3 multiply_add_fusion
  (304 shorter events, 56.4 us)
Async XLA Ops:
  0.6 14.1 %copy-start.4 = (s32[4,8192]{1,0:T(4,128)S(1)}, s32[4,8192]{1,0:T(4,128)}, u32[]{:S(2)}) copy-start(s32[4,8192]{1,0:T(4,128)} %param.21) | copy-start | bytes 393220
  0.6 14.3 %copy-start.6 = (s32[64,128]{1,0:T(8,128)S(1)}, s32[64,128]{1,0:T(8,128)}, u32[]{:S(2)}) copy-start(s32[64,128]{1,0:T(8,128)} %param.26) | copy-start | bytes 98308
  3.7 205.2 %all-to-all-start.2 = ((f32[32,5,128]{2,1,0:T(8,128)}), f32[32,5,128]{2,1,0:T(8,128)S(1)}, u32[]{:S(2)}, u32[]{:S(2)}) async-start(f32[32,5,128]{2,1,0:T(8,128)} %reshape.314), calls=%async_computation.2 | async-start | bytes 262144 | tf_op jit(solution)/shard_map/all_to_all | solution.py:128
  15.1 0.7 copy-start.1
  153.8 19.3 %copy-start = (f32[40960,7]{1,0:T(8,128)S(1)}, f32[40960,7]{1,0:T(8,128)}, u32[]{:S(2)}) copy-start(f32[40960,7]{1,0:T(8,128)} %gather_fusion) | copy-start | bytes 3440644
  197.1 5.9 copy-start.7
  197.1 5.9 copy-start.14
  197.2 6.0 copy-start.8
  202.9 12.4 %copy-start.13 = (s32[512]{0:T(512)S(1)}, s32[512]{0:T(512)}, u32[]{:S(2)}) copy-start(s32[512]{0:T(512)} %param.31) | copy-start | bytes 6148
  202.9 12.4 %copy-start.9 = (s32[2,2048]{1,0:T(2,128)S(1)}, s32[2,2048]{1,0:T(2,128)}, u32[]{:S(2)}) copy-start(s32[2,2048]{1,0:T(2,128)} %param.25) | copy-start | bytes 49156
  204.4 22.5 %copy-start.12 = (s32[512]{0:T(512)S(1)}, s32[512]{0:T(512)}, u32[]{:S(2)}) copy-start(s32[512]{0:T(512)} %param.30) | copy-start | bytes 6148
  208.9 18.0 %all-to-all-start.1 = ((f32[32,5,3,128]{3,2,1,0:T(4,128)}), f32[32,5,3,128]{3,2,1,0:T(4,128)S(1)}, u32[]{:S(2)}, u32[]{:S(2)}) async-start(f32[32,5,3,128]{3,2,1,0:T(4,128)} %bitcast.12), calls=%async_computation.1 | async-start | bytes 655360 | tf_op jit(solution)/shard_map/all_to_all | solution.py:127
  379.3 5.2 copy-start.10
  381.2 15.4 %all-to-all-start.3 = ((f32[32,5,3,128]{3,2,1,0:T(4,128)}), f32[32,5,3,128]{3,2,1,0:T(4,128)}, u32[]{:S(2)}, u32[]{:S(2)}) async-start(f32[32,5,3,128]{3,2,1,0:T(4,128)} %copy.130), calls=%async_computation.3 | async-start | bytes 655360 | tf_op jit(solution)/shard_map/all_to_all | solution.py:142
  385.6 11.1 %copy-start.11 = (s32[160]{0:T(256)S(1)}, s32[160]{0:T(256)}, u32[]{:S(2)}) copy-start(s32[160]{0:T(256)} %eq.98) | copy-start | bytes 1924
  646.1 16.6 %collective-permute-start.1 = (f32[3,2048]{1,0:T(4,128)S(1)}, f32[3,2048]{1,0:T(4,128)S(1)}, u32[]{:S(2)}, u32[]{:S(2)}) collective-permute-start(f32[3,2048]{1,0:T(4,128)S(1)} %copy.134), channel_id=1, source_target_pairs={{1,0},{2,1},{3,2},{4,3},{5,4},{6,5},{7,6},{9,8},{10,9},{11,10},{12... | collective-permute-start | bytes 73736 | tf_op jit(solution)/shard_map/ppermute | solution.py:16
  647.4 43.1 %copy-start.2 = (f32[3,8192]{1,0:T(4,128)S(1)}, f32[3,8192]{1,0:T(4,128)}, u32[]{:S(2)}) copy-start(f32[3,8192]{1,0:T(4,128)} %param.18) | copy-start | bytes 294916
  647.4 43.1 %copy-start.3 = (f32[8192]{0:T(1024)S(1)}, f32[8192]{0:T(1024)}, u32[]{:S(2)}) copy-start(f32[8192]{0:T(1024)} %param.20) | copy-start | bytes 98308
  647.4 43.1 %copy-start.5 = (f32[3,8192]{1,0:T(4,128)S(1)}, f32[3,8192]{1,0:T(4,128)}, u32[]{:S(2)}) copy-start(f32[3,8192]{1,0:T(4,128)} %param.19) | copy-start | bytes 294916
  647.7 15.0 %collective-permute-start = (f32[3,2048]{1,0:T(4,128)S(1)}, f32[3,2048]{1,0:T(4,128)S(1)}, u32[]{:S(2)}, u32[]{:S(2)}) collective-permute-start(f32[3,2048]{1,0:T(4,128)S(1)} %copy.133), channel_id=1, source_target_pairs={{0,1},{1,2},{2,3},{3,4},{4,5},{5,6},{6,7},{8,9},{9,10},{10,11},{11... | collective-permute-start | bytes 73736 | tf_op jit(solution)/shard_map/ppermute | solution.py:16
where the time goes:
time: 693 us; the launch traced here: 692 us
  other arithmetic  367 us (53%)
  local copies, waits for them, and re-layouts  250 us (36%)
  starting transfers between devices  22.4 us (3%)
  waiting for transfers between devices  20.9 us (3%)
  matrix products  10.5 us (2%)
  loops' own time  10.4 us (2%)
  blocking collectives  9.1 us (1%)
    scatter-add x1, other arithmetic, shards(): totals = jnp.zeros_like(displacement).at[:, all_index].add(all_force)  220 us
    gather x1, local copies, waits for them, and re-layouts, shards(): picked = node_rows[:, all_index]  138 us
    reduce_sum x16, other arithmetic, pair_forces(): recoil = -jnp.sum(weights[:, None] * offset, 2)  63.9 us
    reduce_sum x16, other arithmetic, pair_forces(): weights = jnp.exp(-jnp.sum(offset * offset, 1))  33 us
    scatter-add x1, other arithmetic, shards(): totals.at[:, share_flat].add(jnp.concatenate([from_lower, from_upper], 1))  24.2 us
    gather x1, local copies, waits for them, and re-layouts, shards(): share_rows = totals[:, share_flat]  16.3 us
  transfers between devices with their start and end apart: 5, of which 2 were waited for; matrix products, arithmetic and copies ran while one was open for 29% of the time, Pallas kernels for 0%

commit v1 on v0

v1 whole, which is shorter than its diff:
```python
import functools
import math

import jax
import jax.numpy as jnp
from jax import lax
from jax.experimental import pallas as pl
from jax.experimental.pallas import tpu as pltpu
from jax.sharding import PartitionSpec as P

SPRINGS = ((0, 1, 1.0), (1, 2, 1.0), (2, 3, 1.0), (3, 0, 1.0), (0, 2, 0.5), (1, 3, 0.5))
COURANT = 0.5
LOG2E = 1.4426950408889634
FAR_AWAY = 64.0
WIDE = 256
LIMIT = 48 * 1024 * 1024
F32 = jnp.float32
BF16 = jnp.bfloat16
VMEM = pl.BlockSpec(memory_space=pltpu.VMEM)
SMEM = pl.BlockSpec(memory_space=pltpu.SMEM)
PARAMS = pltpu.CompilerParams(vmem_limit_bytes=LIMIT)


def shifted(value, axis, steps):
    count = lax.axis_size(axis)
    first, last = (max(0, -steps), min(count, count - steps))
    return lax.ppermute(value, axis, [(source, source + steps) for source in range(first, last)])


def split3(x):
    first = x.astype(BF16).astype(F32)
    rest = x - first
    second = rest.astype(BF16).astype(F32)
    third = (rest - second).astype(BF16).astype(F32)
    return first, second, third


def split_table(table):
    return jnp.concatenate(split3(table), 0).astype(BF16)


def selectors(index, depth):
    count = index.shape[1]
    low = index & (WIDE - 1)
    high = index // WIDE
    hot = jnp.where(lax.broadcasted_iota(jnp.int32, (WIDE, count), 0) == low, 1.0, 0.0)
    mask = lax.broadcasted_iota(jnp.int32, (depth, count), 0) == high
    return hot.astype(BF16), mask


def pick(table, hot, mask):
    depth = mask.shape[0]
    size = table.shape[0] // 3
    parts = jnp.dot(table, hot, preferred_element_type=F32)
    whole = parts[:size] + parts[size : 2 * size] + parts[2 * size :]
    return [
        jnp.sum(jnp.where(mask, whole[row : row + depth], 0.0), 0, keepdims=True)
        for row in range(0, size, depth)
    ]


def spread(rows, hot, mask):
    firsts, seconds = [], []
    for row in rows:
        first = row.astype(BF16).astype(F32)
        firsts.append(jnp.where(mask, first, 0.0))
        seconds.append(jnp.where(mask, row - first, 0.0))
    stacked = jnp.concatenate(firsts + seconds, 0).astype(BF16)
    sums = lax.dot_general(stacked, hot, (((1,), (1,)), ((), ())), preferred_element_type=F32)
    half = sums.shape[0] // 2
    return sums[:half] + sums[half:]


def lane_row(ref, start, count):
    tile = ref[pl.ds(pl.multiple_of(start, 8), count), :]
    return jnp.concatenate([tile[row : row + 1] for row in range(count)], 1)


def segment_kernel(cap, pos_ref, disp_ref, seg_ref, mask_ref, send_ref, own_ref, out_ref):
    depth = pos_ref.shape[0] // 3
    blocks, width = seg_ref.shape
    table = split_table(pos_ref[...] + disp_ref[...])

    def gather(step, carry):
        start = step * 8
        hot, mask = selectors(lane_row(seg_ref, start, 8), depth)
        live = lane_row(mask_ref, start, 8) > 0
        rows = [jnp.where(live, row, -FAR_AWAY) for row in pick(table, hot, mask)]
        square = rows[0] * rows[0] + rows[1] * rows[1] + rows[2] * rows[2]
        rows += [jnp.ones_like(square), -LOG2E * square]
        for block in range(8):
            lanes = slice(block * width, (block + 1) * width)
            for row in range(5):
                own_ref[start + block, row : row + 1, :] = rows[row][:, lanes]
            own_ref[start + block, 5:8, :] = jnp.zeros((3, width), F32)
        return carry

    lax.fori_loop(0, blocks // 8, gather, 0)

    def send(peer, carry):
        for slot in range(cap):
            block = own_ref[send_ref[peer * cap + slot], 0:3, :]
            out_ref[peer, 3 * slot : 3 * slot + 3, :] = jnp.where(
                block < -0.5 * FAR_AWAY, FAR_AWAY, block
            )
        out_ref[peer, 3 * cap :, :] = jnp.zeros((out_ref.shape[1] - 3 * cap, width), F32)
        return carry

    lax.fori_loop(0, out_ref.shape[0], send, 0)


def element_kernel(
    chunk, disp_ref, mass_ref, nodes_ref, part_ref, scale_ref, stiff_ref, force_ref, ratio_ref
):
    depth = mass_ref.shape[0]
    elems = nodes_ref.shape[1]
    parts = stiff_ref.shape[0]
    table = split_table(jnp.concatenate([disp_ref[...], mass_ref[...]], 0))
    force_ref[...] = jnp.zeros_like(force_ref)

    def one_chunk(step, best):
        lanes = pl.ds(pl.multiple_of(step * chunk, chunk), chunk)
        local = lax.rem(part_ref[:, lanes], parts)
        stiff = jnp.zeros(local.shape, F32)
        for part in range(parts):
            stiff = jnp.where(local == part, stiff_ref[part], stiff)
        stiff = stiff * scale_ref[:, lanes]
        index = jnp.concatenate([nodes_ref[k : k + 1, lanes] for k in range(4)], 1)
        hot, mask = selectors(index, depth)
        rows = pick(table, hot, mask)
        corner = [[row[:, k * chunk : (k + 1) * chunk] for row in rows] for k in range(4)]
        mass = jnp.minimum(
            jnp.minimum(corner[0][3], corner[1][3]), jnp.minimum(corner[2][3], corner[3][3])
        )
        total = [[jnp.zeros_like(stiff) for axis in range(3)] for k in range(4)]
        for head, tail, weight in SPRINGS:
            for axis in range(3):
                pull = weight * stiff * (corner[tail][axis] - corner[head][axis])
                total[head][axis] = total[head][axis] + pull
                total[tail][axis] = total[tail][axis] - pull
        rows = [jnp.concatenate([total[k][axis] for k in range(4)], 1) for axis in range(3)]
        force_ref[...] += spread(rows, hot, mask)
        return jnp.minimum(best, mass / stiff)

    best = lax.fori_loop(
        0, elems // chunk, one_chunk, jnp.full((1, chunk), jnp.inf, F32)
    )
    ratio_ref[...] = jnp.broadcast_to(jnp.min(best, 1, keepdims=True), ratio_ref.shape)


def pair_kernel(
    cap,
    group,
    own_ref,
    got_ref,
    ratio_ref,
    first_ref,
    second_ref,
    live_ref,
    seg_ref,
    back_ref,
    near_turn,
    near_cols,
    far_rows,
    far_cols,
    near_sum,
    far_sum,
    tile_ref,
):
    blocks, _, width = own_ref.shape
    peers = got_ref.shape[0]
    pairs = first_ref.shape[0]

    def doubled(parts):
        stacked = jnp.concatenate(parts + [jnp.zeros_like(parts[0])], 0)
        return jnp.concatenate([stacked, stacked], 1).astype(BF16)

    def prepare_near(block, carry):
        one, two, three = split3(own_ref[block])
        near_turn[block] = jnp.concatenate([one, one, two, two, one, three], 0).T.astype(BF16)
        near_cols[block] = doubled([one, two, three])
        near_sum[block] = jnp.zeros((8, width), F32)
        return carry

    lax.fori_loop(0, blocks, prepare_near, 0)

    row_id = lax.broadcasted_iota(jnp.int32, (8, width), 0)
    tile_ref[...] = jnp.zeros_like(tile_ref)

    def prepare_far(peer, carry):
        for slot in range(cap):
            tile_ref[slot, 0:3, :] = got_ref[peer, 3 * slot : 3 * slot + 3, :]
        for slot in range(cap):
            tile = tile_ref[slot]
            square = -LOG2E * jnp.sum(tile * tile, 0, keepdims=True)
            scaled = jnp.where(
                row_id == 3, square, jnp.where(row_id == 4, 1.0, (2.0 * LOG2E) * tile)
            )
            one, two, three = split3(scaled)
            place = peer * cap + slot
            far_rows[place] = jnp.concatenate([one, two, one, two, three, one], 0).astype(BF16)
            far_cols[place] = doubled(list(split3(jnp.where(row_id == 3, 1.0, tile))))
            far_sum[place] = jnp.zeros((8, width), F32)
        return carry

    lax.fori_loop(0, peers, prepare_far, 0)

    def one_group(step, carry):
        results = []
        for member in range(group):
            place = step * group + member
            near, far = first_ref[place], second_ref[place]
            live = live_ref[place].astype(F32)
            power = jnp.dot(near_turn[near], far_rows[far], preferred_element_type=F32)
            weight = jnp.exp2(power)
            first = weight.astype(BF16)
            second = (weight - first.astype(F32)).astype(BF16)
            pushed = lax.dot_general(
                far_cols[far],
                jnp.concatenate([first, second], 1),
                (((1,), (1,)), ((), ())),
                preferred_element_type=F32,
            )
            recoil = jnp.dot(
                near_cols[near],
                jnp.concatenate([first, second], 0),
                preferred_element_type=F32,
            )
            pushed = live * (pushed[0:8] + pushed[8:16] + pushed[16:24])
            recoil = live * (recoil[0:8] + recoil[8:16] + recoil[16:24])
            results.append((near, far, pushed, recoil))
        for near, far, pushed, recoil in results:
            near_sum[near] += pushed
            far_sum[far] += recoil
        return carry

    lax.fori_loop(0, pairs // group, one_group, 0)

    def finish_near(block, carry):
        sums = near_sum[block]
        seg_ref[block] = own_ref[block] * sums[3:4] - sums
        return carry

    lax.fori_loop(0, blocks, finish_near, 0)

    def finish_far(peer, carry):
        for slot in range(cap):
            rows = slice(3 * slot, 3 * slot + 3)
            sums = far_sum[peer * cap + slot]
            back_ref[peer, rows, :] = got_ref[peer, rows, :] * sums[3:4] - sums[0:3]
        back_ref[peer, 3 * cap :, :] = jnp.broadcast_to(
            ratio_ref[0:1], (back_ref.shape[1] - 3 * cap, width)
        )
        return carry

    lax.fori_loop(0, peers, finish_far, 0)


def total_kernel(
    cap,
    chunk,
    back_ref,
    send_ref,
    own_ref,
    seg_ref,
    force_ref,
    shared_ref,
    total_ref,
    lower_ref,
    upper_ref,
    step_ref,
    sums,
):
    depth = force_ref.shape[0] // 3
    blocks, width = seg_ref.shape
    sums[...] = own_ref[...]

    def give_back(peer, best):
        for slot in range(cap):
            block = send_ref[peer * cap + slot]
            sums[block, 0:3, :] += back_ref[peer, 3 * slot : 3 * slot + 3, :]
        return jnp.minimum(best, back_ref[peer, 3 * cap : 3 * cap + 1, :])

    best = lax.fori_loop(
        0, back_ref.shape[0], give_back, jnp.full((1, width), jnp.inf, F32)
    )
    step_ref[...] = jnp.broadcast_to(COURANT * jnp.sqrt(best), step_ref.shape)
    total_ref[...] = force_ref[...]

    def scatter(step, carry):
        start = step * 8
        hot, mask = selectors(lane_row(seg_ref, start, 8), depth)
        rows = [
            jnp.concatenate([sums[start + block, row : row + 1, :] for block in range(8)], 1)
            for row in range(3)
        ]
        total_ref[...] += spread(rows, hot, mask)
        return carry

    lax.fori_loop(0, blocks // 8, scatter, 0)

    table = split_table(total_ref[...])

    def gather(step, carry):
        lanes = pl.ds(pl.multiple_of(step * chunk, chunk), chunk)
        for side, out_ref in ((0, upper_ref), (1, lower_ref)):
            hot, mask = selectors(shared_ref[side : side + 1, lanes], depth)
            rows = pick(table, hot, mask)
            for row in range(3):
                out_ref[row : row + 1, lanes] = rows[row]
        return carry

    lax.fori_loop(0, shared_ref.shape[1] // chunk, gather, 0)


def update_kernel(
    chunk,
    total_ref,
    lower_ref,
    upper_ref,
    shared_ref,
    mass_ref,
    vel_ref,
    disp_ref,
    step_ref,
    new_disp_ref,
    new_vel_ref,
):
    depth = mass_ref.shape[0]
    new_vel_ref[...] = total_ref[...]

    def scatter(step, carry):
        lanes = pl.ds(pl.multiple_of(step * chunk, chunk), chunk)
        for side, in_ref in ((0, lower_ref), (1, upper_ref)):
            hot, mask = selectors(shared_ref[side : side + 1, lanes], depth)
            rows = [in_ref[row : row + 1, lanes] for row in range(3)]
            new_vel_ref[...] += spread(rows, hot, mask)
        return carry

    lax.fori_loop(0, shared_ref.shape[1] // chunk, scatter, 0)
    time_step = step_ref[0:1, 0:1]
    mass = mass_ref[...]
    for axis in range(3):
        rows = slice(axis * depth, (axis + 1) * depth)
        velocity = vel_ref[rows, :] + time_step * (new_vel_ref[rows, :] / mass)
        new_vel_ref[rows, :] = velocity
        new_disp_ref[rows, :] = disp_ref[rows, :] + time_step * velocity


def shape(*dims):
    return jax.ShapeDtypeStruct(dims, F32)


def shards(
    ref_pos,
    displacement,
    velocity,
    node_mass,
    elem_nodes,
    elem_part,
    elem_scale,
    part_stiff,
    shared,
    seg_node,
    seg_mask,
    send_blk,
    pair_a,
    pair_slot,
    pair_mask,
):
    axes = ("grp", "dev")
    peers, cap = send_blk.shape[1:]
    nodes = node_mass.shape[0]
    blocks, width = seg_node.shape
    elems = elem_nodes.shape[1]
    pairs = pair_a.shape[0]
    share = shared.shape[1]
    depth = nodes // WIDE
    slab = -(-(3 * cap + 1) // 8) * 8
    pos = ref_pos.reshape(3 * depth, WIDE)
    disp = displacement.reshape(3 * depth, WIDE)
    mass = node_mass.reshape(depth, WIDE)
    send = send_blk.reshape(-1)

    own, outgoing = pl.pallas_call(
        functools.partial(segment_kernel, cap),
        out_shape=(shape(blocks, 8, width), shape(peers, slab, width)),
        in_specs=[VMEM, VMEM, VMEM, VMEM, SMEM],
        out_specs=(VMEM, VMEM),
        compiler_params=PARAMS,
        name="segments",
    )(pos, disp, seg_node, seg_mask, send)
    arrived = lax.all_to_all(outgoing, axes, split_axis=0, concat_axis=0, tiled=True)

    chunk = math.gcd(elems, 512)
    force, ratio = pl.pallas_call(
        functools.partial(element_kernel, chunk),
        out_shape=(shape(3 * depth, WIDE), shape(8, width)),
        in_specs=[VMEM, VMEM, VMEM, VMEM, VMEM, SMEM],
        out_specs=(VMEM, VMEM),
        compiler_params=PARAMS,
        cost_estimate=pl.CostEstimate(
            flops=2 * 4 * elems * WIDE * depth * 18, bytes_accessed=2**20, transcendentals=0
        ),
        name="elements",
    )(disp, mass, elem_nodes, elem_part.reshape(1, -1), elem_scale.reshape(1, -1), part_stiff)

    group = math.gcd(pairs, 8)
    seg_force, going_back = pl.pallas_call(
        functools.partial(pair_kernel, cap, group),
        out_shape=(shape(blocks, 8, width), shape(peers, slab, width)),
        in_specs=[VMEM, VMEM, VMEM, SMEM, SMEM, SMEM],
        out_specs=(VMEM, VMEM),
        scratch_shapes=[
            pltpu.VMEM((blocks, width, 48), BF16),
            pltpu.VMEM((blocks, 32, 2 * width), BF16),
            pltpu.VMEM((peers * cap, 48, width), BF16),
            pltpu.VMEM((peers * cap, 32, 2 * width), BF16),
            pltpu.VMEM((blocks, 8, width), F32),
            pltpu.VMEM((peers * cap, 8, width), F32),
            pltpu.VMEM((cap, 8, width), F32),
        ],
        compiler_params=PARAMS,
        name="pairs",
    )(own, arrived, ratio, pair_a, pair_slot, pair_mask)
    returned = lax.all_to_all(going_back, axes, split_axis=0, concat_axis=0, tiled=True)

    piece = math.gcd(share, 1024)
    total, lower, upper, time_step = pl.pallas_call(
        functools.partial(total_kernel, cap, piece),
        out_shape=(shape(3 * depth, WIDE), shape(3, share), shape(3, share), shape(8, width)),
        in_specs=[VMEM, SMEM, VMEM, VMEM, VMEM, VMEM],
        out_specs=(VMEM, VMEM, VMEM, VMEM),
        scratch_shapes=[pltpu.VMEM((blocks, 8, width), F32)],
        compiler_params=PARAMS,
        name="totals",
    )(returned, send, seg_force, seg_node, force, shared)
    from_lower = shifted(lower, "dev", 1)
    from_upper = shifted(upper, "dev", -1)

    new_disp, new_vel = pl.pallas_call(
        functools.partial(update_kernel, piece),
        out_shape=(shape(3 * depth, WIDE), shape(3 * depth, WIDE)),
        in_specs=[VMEM] * 8,
        out_specs=(VMEM, VMEM),
        compiler_params=PARAMS,
        name="update",
    )(total, from_lower, from_upper, shared, mass, velocity.reshape(3 * depth, WIDE), disp, time_step)
    return (new_disp.reshape(3, nodes), new_vel.reshape(3, nodes))


def solution(mesh):
    return jax.shard_map(
        shards,
        mesh=mesh,
        in_specs=(
            P(None, ("grp", "dev")),
            P(None, ("grp", "dev")),
            P(None, ("grp", "dev")),
            P(("grp", "dev")),
            P(None, ("grp", "dev")),
            P(("grp", "dev")),
            P(("grp", "dev")),
            P(("grp", "dev")),
            P(None, ("grp", "dev")),
            P(("grp", "dev"), None),
            P(("grp", "dev"), None),
            P(("grp", "dev"), None, None),
            P(("grp", "dev")),
            P(("grp", "dev")),
            P(("grp", "dev")),
        ),
        out_specs=(P(None, ("grp", "dev")), P(None, ("grp", "dev"))),
        check_vma=False,
    )
```

time: 693 us -> 168 us (0.24)
  other arithmetic: 367 us -> 0 us
  local copies, waits for them, and re-layouts: 250 us -> 4.89 us
  Pallas kernels: 0 us -> 130 us
  waiting for transfers between devices: 20.9 us -> 4.42 us
  starting transfers between devices: 22.4 us -> 11.5 us
  matrix products: 10.5 us -> 0 us
  loops' own time: 10.4 us -> 0 us
  blocking collectives: 9.1 us -> 16.3 us
    scatter-add x2 -> x0, other arithmetic: 244 us -> none  [the longest x1 220 us: shards(): totals = jnp.zeros_like(displacement).at[:, all_index].add(all_force)]
    gather x5 -> x0, local copies, waits for them, and re-layouts: 157 us -> none  [the longest x1 138 us: shards(): picked = node_rows[:, all_index]]
    pallas_call x0 -> x5, Pallas kernels: none -> 130 us  [the longest x1 95.4 us: shards(): pl.pallas_call(functools.partial(pair_kernel, cap, group), out_shape=(sha...]
    reduce_sum x33 -> x0, other arithmetic: 97 us -> none  [the longest x16 63.9 us: pair_forces(): recoil = -jnp.sum(weights[:, None] * offset, 2)]
    slice x70 -> x0, local copies, waits for them, and re-layouts: 33.6 us -> none  [the longest x1 12.7 us: shards(): elem_mass = jnp.min(picked[3, :4 * elem_count].reshape(4, elem_count), 0)]
    dynamic_slice x64 -> x0, local copies, waits for them, and re-layouts: 23.9 us -> none  [the longest x16 12.2 us: one_group(): first_ids = lax.dynamic_slice_in_dim(pair_first, group_start, group_width)]
    all_to_all x3 -> x1, waiting for transfers between devices: 20.9 us -> 0.01 us  [shards(): lax.all_to_all(outgoing, axes, split_axis=0, concat_axis=0, tiled=True)]
    concatenate x3 -> x0, local copies, waits for them, and re-layouts: 13.3 us -> none  [the longest x1 10 us: shards(): all_force = jnp.concatenate([stacked.reshape(3, -1), flat_force], 1)]
  transfers between devices with their start and end apart: 5 -> 3, of which waited for: 2 -> 2; matrix products, arithmetic and copies ran while one was open for 29% -> 0% of each run, Pallas kernels for 0% -> 14%
where the time goes in v1:
time: 168 us
  Pallas kernels  130 us (77%)
  blocking collectives  16.3 us (10%)
  starting transfers between devices  11.5 us (7%)
  local copies, waits for them, and re-layouts  4.89 us (3%)
  waiting for transfers between devices  4.42 us (3%)
    pallas_call x1, Pallas kernels, shards(): pl.pallas_call(functools.partial(pair_kernel, cap, group), out_shape=(sha...  95.4 us
    pallas_call x1, Pallas kernels, shards(): pl.pallas_call(functools.partial(element_kernel, chunk), out_shape=(shape...  24 us
    all_to_all x1, blocking collectives, shards(): lax.all_to_all(going_back, axes, split_axis=0, concat_axis=0, tiled=True)  16.3 us
    all_to_all x1, starting transfers between devices, shards(): lax.all_to_all(outgoing, axes, split_axis=0, concat_axis=0, tiled=True)  7.3 us
    pallas_call x1, Pallas kernels, shards(): pl.pallas_call(functools.partial(total_kernel, cap, piece), out_shape=(sh...  5.05 us
    ppermute x2, waiting for transfers between devices, shifted(): lax.ppermute(value, axis, [(source, source + steps) for source in range(f...  4.41 us
    pallas_call x1, Pallas kernels, shards(): pl.pallas_call(functools.partial(segment_kernel, cap), out_shape=(shape(b...  4.34 us
    ppermute x2, starting transfers between devices, shifted(): lax.ppermute(value, axis, [(source, source + steps) for source in range(f...  4.2 us
  transfers between devices with their start and end apart: 3, of which 2 were waited for; matrix products, arithmetic and copies ran while one was open for 0% of the time, Pallas kernels for 14%

profile of v1, /device:TPU:0, one launch (start us, length us, event | category | flops | bytes accessed | tf_op | source)
XLA Modules:
  0.0 167.9 jit_solution(11074621524834356518)
XLA Ops:
  0.6 0.0 copy-start.13
  0.6 0.0 copy-start.10
  0.6 1.0 reshape.32.disp_ref
  1.7 0.0 copy-done.13
  1.7 0.1 copy.17
  1.8 0.1 reshape.33.send_ref
  1.9 0.0 copy-done.10
  1.9 0.0 copy-start
  1.9 0.0 copy-start.2
  1.9 0.1 reshape.31.pos_ref
  2.0 0.7 copy-done
  2.6 0.0 copy-done.2
  2.7 4.3 %segments.1 = (f32[64,8,128]{2,1,0:T(8,128)S(1)}, f32[32,16,128]{2,1,0:T(8,128)}) custom-call(f32[96,256]{1,0:T(8,128)S(1)} %reshape.31.pos_ref, f32[96,256]{1,0:T(8,128)S(1)} %reshape.32.disp_ref, s32[64,128]{1,0:T(8,128)S(1)} %copy-done, s32[64,128]{1,0:T(8,128)S(1)} %copy-done.2, s32[160]{0:T(256)S(1)} %reshape.33.send_ref), custom_call_target="tpu_custom_call" | custom-call | tf_op jit(solution)/shard_map/segments/pallas_call | solution.py:385
  7.0 0.0 copy-start.12
  7.0 0.0 copy-start.6
  7.0 7.3 %all-to-all-start = ((f32[32,16,128]{2,1,0:T(8,128)}), f32[32,16,128]{2,1,0:T(8,128)S(1)}, u32[]{:S(2)}, u32[]{:S(2)}) async-start(f32[32,16,128]{2,1,0:T(8,128)} %get-tuple-element.15), calls=%async_computation | async-start | bytes 524288 | tf_op jit(solution)/shard_map/all_to_all | solution.py:393
  14.3 0.0 copy-done.12
  14.3 0.0 copy-start.7
  14.3 0.0 copy-start.8
  14.4 0.0 copy-start.9
  14.4 0.0 copy-done.6
  14.4 0.7 copy-done.7
  15.1 0.0 copy-done.8
  15.1 0.0 copy-done.9
  15.1 0.0 copy-start.4
  15.1 0.0 copy-start.5
  15.1 24.0 %elements.1 = (f32[96,256]{1,0:T(8,128)S(1)}, f32[8,128]{1,0:T(8,128)S(1)}) custom-call(f32[96,256]{1,0:T(8,128)S(1)} %reshape.32.disp_ref, f32[32,256]{1,0:T(8,128)S(1)} %reshape.34.mass_ref, s32[4,8192]{1,0:T(4,128)S(1)} %copy-done.6, s32[1,8192]{1,0:T(1,128)S(1)} %bitcast.2, f32[1,8192]{1,0:T(1,128)S(1)} %bitcast.3, f32[4]{0:T(128)S(1)} %copy-done.9), custom_call_target="tpu_custom_call" | custom-call | flops 9663676416 | bytes 1048576 | tf_op jit(solution)/shard_map/elements/pallas_call | solution.py:396
  39.1 0.0 copy-start.3
  39.1 0.0 all-to-all-done.got_ref
  39.1 0.0 copy-done.4
  39.2 0.0 copy-done.5
  39.2 0.7 copy-done.3
  39.8 95.4 %pairs.1 = (f32[64,8,128]{2,1,0:T(8,128)S(1)}, f32[32,16,128]{2,1,0:T(8,128)S(1)}) custom-call(f32[64,8,128]{2,1,0:T(8,128)S(1)} %get-tuple-element.14.own_ref, f32[32,16,128]{2,1,0:T(8,128)S(1)} %all-to-all-done.got_ref, f32[8,128]{1,0:T(8,128)S(1)} %get-tuple-element.16.ratio_ref, s32[512]{0:T(512)S(1)} %copy-done.3, s32[512]{0:T(512)S(1)} %copy-done.4, ...), custom_call_target="tpu_custom_call" | custom-call | tf_op jit(solution)/shard_map/pairs/pallas_call | solution.py:409
  135.3 0.0 copy-start.1
  135.3 16.3 %all_to_all.10.back_ref = f32[32,16,128]{2,1,0:T(8,128)S(1)} all-to-all(f32[32,16,128]{2,1,0:T(8,128)S(1)} %get-tuple-element.17), channel_id=1, replica_groups=mesh['grp'=4,'dev'=8] {'grp','dev'}, dimensions={0} | all-to-all | bytes 524288 | tf_op jit(solution)/shard_map/all_to_all | solution.py:426
  151.6 0.0 copy-done.1
  151.6 0.0 copy-start.11
  151.6 5.0 %totals.1 = (f32[96,256]{1,0:T(8,128)S(1)}, f32[3,2048]{1,0:T(4,128)S(1)}, f32[3,2048]{1,0:T(4,128)S(1)}, f32[8,128]{1,0:T(8,128)S(1)}) custom-call(f32[32,16,128]{2,1,0:T(8,128)S(1)} %all_to_all.10.back_ref, s32[160]{0:T(256)S(1)} %reshape.33.send_ref, f32[64,8,128]{2,1,0:T(8,128)S(1)} %get-tuple-element.18.own_ref, s32[64,128]{1,0:T(8,128)S(1)} %copy-done, ...), custom_call_target="tpu_custom_call" | custom-call | tf_op jit(solution)/shard_map/totals/pallas_call | solution.py:429
  156.7 2.9 %collective-permute-start = (f32[3,2048]{1,0:T(4,128)S(1)}, f32[3,2048]{1,0:T(4,128)S(1)}, u32[]{:S(2)}, u32[]{:S(2)}) collective-permute-start(f32[3,2048]{1,0:T(4,128)S(1)} %get-tuple-element.21), channel_id=1, source_target_pairs={{0,1},{1,2},{2,3},{3,4},{4,5},{5,6},{6,7},{8,9},{9,10},{10,11},{11... | collective-permute-start | bytes 73736 | tf_op jit(solution)/shard_map/ppermute | solution.py:27
  159.6 1.3 collective-permute-start.1
  160.9 0.0 copy-done.11
  160.9 0.1 reshape.37.vel_ref
  161.0 0.2 collective-permute-done.lower_ref
  161.2 4.2 %collective-permute-done.1.upper_ref = f32[3,2048]{1,0:T(4,128)S(1)} collective-permute-done((f32[3,2048]{1,0:T(4,128)S(1)}, f32[3,2048]{1,0:T(4,128)S(1)}, u32[]{:S(2)}, u32[]{:S(2)}) %collective-permute-start.1) | collective-permute-done | bytes 24608 | tf_op jit(solution)/shard_map/ppermute | solution.py:27
  165.4 1.1 update.1
  166.5 0.7 reshape.38
  167.2 0.7 reshape.39
  (1 shorter events, 0.0 us)
Async XLA Ops:
  0.6 1.0 copy-start.13
  0.6 1.2 copy-start.10
  1.9 0.8 copy-start
  1.9 0.8 copy-start.2
  7.0 7.3 %copy-start.12 = (f32[8192]{0:T(1024)S(1)}, f32[8192]{0:T(1024)}, u32[]{:S(2)}) copy-start(f32[8192]{0:T(1024)} %param.18) | copy-start | bytes 98308
  7.0 7.4 %copy-start.6 = (s32[4,8192]{1,0:T(4,128)S(1)}, s32[4,8192]{1,0:T(4,128)}, u32[]{:S(2)}) copy-start(s32[4,8192]{1,0:T(4,128)} %nodes_ref.1) | copy-start | bytes 393220
  7.0 32.1 %all-to-all-start = ((f32[32,16,128]{2,1,0:T(8,128)}), f32[32,16,128]{2,1,0:T(8,128)S(1)}, u32[]{:S(2)}, u32[]{:S(2)}) async-start(f32[32,16,128]{2,1,0:T(8,128)} %get-tuple-element.15), calls=%async_computation | async-start | bytes 524288 | tf_op jit(solution)/shard_map/all_to_all | solution.py:393
  14.3 0.8 copy-start.7
  14.3 0.8 copy-start.8
  14.4 0.7 copy-start.9
  15.1 24.0 %copy-start.4 = (s32[512]{0:T(512)S(1)}, s32[512]{0:T(512)}, u32[]{:S(2)}) copy-start(s32[512]{0:T(512)} %second_ref.1) | copy-start | bytes 6148
  15.1 24.0 %copy-start.5 = (s32[512]{0:T(512)S(1)}, s32[512]{0:T(512)}, u32[]{:S(2)}) copy-start(s32[512]{0:T(512)} %live_ref.1) | copy-start | bytes 6148
  39.1 0.7 copy-start.3
  135.3 16.4 %copy-start.1 = (s32[2,2048]{1,0:T(2,128)S(1)}, s32[2,2048]{1,0:T(2,128)}, u32[]{:S(2)}) copy-start(s32[2,2048]{1,0:T(2,128)} %shared_ref.3) | copy-start | bytes 49156
  151.6 9.3 %copy-start.11 = (f32[3,8192]{1,0:T(4,128)S(1)}, f32[3,8192]{1,0:T(4,128)}, u32[]{:S(2)}) copy-start(f32[3,8192]{1,0:T(4,128)} %param.17) | copy-start | bytes 294916
  156.7 4.5 %collective-permute-start = (f32[3,2048]{1,0:T(4,128)S(1)}, f32[3,2048]{1,0:T(4,128)S(1)}, u32[]{:S(2)}, u32[]{:S(2)}) collective-permute-start(f32[3,2048]{1,0:T(4,128)S(1)} %get-tuple-element.21), channel_id=1, source_target_pairs={{0,1},{1,2},{2,3},{3,4},{4,5},{5,6},{6,7},{8,9},{9,10},{10,11},{11... | collective-permute-start | bytes 73736 | tf_op jit(solution)/shard_map/ppermute | solution.py:27
  159.6 5.8 %collective-permute-start.1 = (f32[3,2048]{1,0:T(4,128)S(1)}, f32[3,2048]{1,0:T(4,128)S(1)}, u32[]{:S(2)}, u32[]{:S(2)}) collective-permute-start(f32[3,2048]{1,0:T(4,128)S(1)} %get-tuple-element.22), channel_id=1, source_target_pairs={{1,0},{2,1},{3,2},{4,3},{5,4},{6,5},{7,6},{9,8},{10,9},{11,10},{12... | collective-permute-start | bytes 73736 | tf_op jit(solution)/shard_map/ppermute | solution.py:27

commit v2 on v1

--- a/solution.py
+++ b/solution.py
@@ -13,7 +13,7 @@
 LOG2E = 1.4426950408889634
 FAR_AWAY = 64.0
 WIDE = 256
-LIMIT = 48 * 1024 * 1024
+LIMIT = 56 * 1024 * 1024
 F32 = jnp.float32
 BF16 = jnp.bfloat16
 VMEM = pl.BlockSpec(memory_space=pltpu.VMEM)
@@ -109,14 +109,13 @@
     lax.fori_loop(0, out_ref.shape[0], send, 0)
 
 
-def element_kernel(
-    chunk, disp_ref, mass_ref, nodes_ref, part_ref, scale_ref, stiff_ref, force_ref, ratio_ref
+def pull_kernel(
+    chunk, disp_ref, mass_ref, nodes_ref, part_ref, scale_ref, stiff_ref, pull_ref, ratio_ref
 ):
     depth = mass_ref.shape[0]
     elems = nodes_ref.shape[1]
     parts = stiff_ref.shape[0]
     table = split_table(jnp.concatenate([disp_ref[...], mass_ref[...]], 0))
-    force_ref[...] = jnp.zeros_like(force_ref)
 
     def one_chunk(step, best):
         lanes = pl.ds(pl.multiple_of(step * chunk, chunk), chunk)
@@ -138,14 +137,33 @@
                 pull = weight * stiff * (corner[tail][axis] - corner[head][axis])
                 total[head][axis] = total[head][axis] + pull
                 total[tail][axis] = total[tail][axis] - pull
-        rows = [jnp.concatenate([total[k][axis] for k in range(4)], 1) for axis in range(3)]
-        force_ref[...] += spread(rows, hot, mask)
+        for axis in range(3):
+            for k in range(4):
+                pull_ref[4 * axis + k : 4 * axis + k + 1, lanes] = total[k][axis]
         return jnp.minimum(best, mass / stiff)
 
     best = lax.fori_loop(
         0, elems // chunk, one_chunk, jnp.full((1, chunk), jnp.inf, F32)
     )
     ratio_ref[...] = jnp.broadcast_to(jnp.min(best, 1, keepdims=True), ratio_ref.shape)
+
+
+def force_kernel(chunk, pull_ref, nodes_ref, after_ref, force_ref):
+    depth = force_ref.shape[0] // 3
+    force_ref[...] = jnp.zeros_like(force_ref)
+
+    def one_chunk(step, carry):
+        lanes = pl.ds(pl.multiple_of(step * chunk, chunk), chunk)
+        index = jnp.concatenate([nodes_ref[k : k + 1, lanes] for k in range(4)], 1)
+        hot, mask = selectors(index, depth)
+        rows = [
+            jnp.concatenate([pull_ref[4 * axis + k : 4 * axis + k + 1, lanes] for k in range(4)], 1)
+            for axis in range(3)
+        ]
+        force_ref[...] += spread(rows, hot, mask)
+        return carry
+
+    lax.fori_loop(0, nodes_ref.shape[1] // chunk, one_chunk, 0)
 
 
 def pair_kernel(
@@ -159,9 +177,11 @@
     live_ref,
     seg_ref,
     back_ref,
+    near_rows,
     near_turn,
     near_cols,
     far_rows,
+    far_turn,
     far_cols,
     near_sum,
     far_sum,
@@ -170,19 +190,24 @@
     blocks, _, width = own_ref.shape
     peers = got_ref.shape[0]
     pairs = first_ref.shape[0]
+    scale = 2.0 * LOG2E
 
     def doubled(parts):
         stacked = jnp.concatenate(parts + [jnp.zeros_like(parts[0])], 0)
         return jnp.concatenate([stacked, stacked], 1).astype(BF16)
 
-    def prepare_near(block, carry):
-        one, two, three = split3(own_ref[block])
-        near_turn[block] = jnp.concatenate([one, one, two, two, one, three], 0).T.astype(BF16)
-        near_cols[block] = doubled([one, two, three])
-        near_sum[block] = jnp.zeros((8, width), F32)
-        return carry
-
-    lax.fori_loop(0, blocks, prepare_near, 0)
+    def prepare_near(step, carry):
+        for member in range(8):
+            block = 8 * step + member
+            one, two, three = split3(own_ref[block])
+            rows = jnp.concatenate([one, one, two, two, one, three], 0)
+            near_rows[block] = rows.astype(BF16)
+            near_turn[block] = rows.T.astype(BF16)
+            near_cols[block] = doubled([one, two, three])
+            near_sum[block] = jnp.zeros((8, width), F32)
+        return carry
+
+    lax.fori_loop(0, blocks // 8, prepare_near, 0)
 
     row_id = lax.broadcasted_iota(jnp.int32, (8, width), 0)
     tile_ref[...] = jnp.zeros_like(tile_ref)
@@ -193,17 +218,24 @@
         for slot in range(cap):
             tile = tile_ref[slot]
             square = -LOG2E * jnp.sum(tile * tile, 0, keepdims=True)
-            scaled = jnp.where(
-                row_id == 3, square, jnp.where(row_id == 4, 1.0, (2.0 * LOG2E) * tile)
+            one, two, three = split3(
+                jnp.where(row_id == 3, square, jnp.where(row_id == 4, 1.0, scale * tile))
             )
-            one, two, three = split3(scaled)
             place = peer * cap + slot
-            far_rows[place] = jnp.concatenate([one, two, one, two, three, one], 0).astype(BF16)
-            far_cols[place] = doubled(list(split3(jnp.where(row_id == 3, 1.0, tile))))
+            rows = jnp.concatenate([one, two, one, two, three, one], 0)
+            far_rows[place] = rows.astype(BF16)
+            far_turn[place] = rows.T.astype(BF16)
+            far_cols[place] = doubled([one, two, three])
             far_sum[place] = jnp.zeros((8, width), F32)
         return carry
 
     lax.fori_loop(0, peers, prepare_far, 0)
+
+    def weights(left, right):
+        weight = jnp.exp2(jnp.dot(left, right, preferred_element_type=F32))
+        first = weight.astype(BF16)
+        second = (weight - first.astype(F32)).astype(BF16)
+        return jnp.concatenate([first, second], 0)
 
     def one_group(step, carry):
         results = []
@@ -211,20 +243,11 @@
             place = step * group + member
             near, far = first_ref[place], second_ref[place]
             live = live_ref[place].astype(F32)
-            power = jnp.dot(near_turn[near], far_rows[far], preferred_element_type=F32)
-            weight = jnp.exp2(power)
-            first = weight.astype(BF16)
-            second = (weight - first.astype(F32)).astype(BF16)
-            pushed = lax.dot_general(
-                far_cols[far],
-                jnp.concatenate([first, second], 1),
-                (((1,), (1,)), ((), ())),
-                preferred_element_type=F32,
+            pushed = jnp.dot(
+                far_cols[far], weights(far_turn[far], near_rows[near]), preferred_element_type=F32
             )
             recoil = jnp.dot(
-                near_cols[near],
-                jnp.concatenate([first, second], 0),
-                preferred_element_type=F32,
+                near_cols[near], weights(near_turn[near], far_rows[far]), preferred_element_type=F32
             )
             pushed = live * (pushed[0:8] + pushed[8:16] + pushed[16:24])
             recoil = live * (recoil[0:8] + recoil[8:16] + recoil[16:24])
@@ -236,12 +259,14 @@
 
     lax.fori_loop(0, pairs // group, one_group, 0)
 
-    def finish_near(block, carry):
-        sums = near_sum[block]
-        seg_ref[block] = own_ref[block] * sums[3:4] - sums
-        return carry
-
-    lax.fori_loop(0, blocks, finish_near, 0)
+    def finish_near(step, carry):
+        for member in range(8):
+            block = 8 * step + member
+            sums = near_sum[block]
+            seg_ref[block] = own_ref[block] * sums[4:5] - (1.0 / scale) * sums
+        return carry
+
+    lax.fori_loop(0, blocks // 8, finish_near, 0)
 
     def finish_far(peer, carry):
         for slot in range(cap):
@@ -393,16 +418,15 @@
     arrived = lax.all_to_all(outgoing, axes, split_axis=0, concat_axis=0, tiled=True)
 
     chunk = math.gcd(elems, 512)
-    force, ratio = pl.pallas_call(
-        functools.partial(element_kernel, chunk),
-        out_shape=(shape(3 * depth, WIDE), shape(8, width)),
+    work = 2 * 4 * elems * WIDE * depth
+    pull, ratio = pl.pallas_call(
+        functools.partial(pull_kernel, chunk),
+        out_shape=(shape(12, elems), shape(8, width)),
         in_specs=[VMEM, VMEM, VMEM, VMEM, VMEM, SMEM],
         out_specs=(VMEM, VMEM),
         compiler_params=PARAMS,
-        cost_estimate=pl.CostEstimate(
-            flops=2 * 4 * elems * WIDE * depth * 18, bytes_accessed=2**20, transcendentals=0
-        ),
-        name="elements",
+        cost_estimate=pl.CostEstimate(flops=12 * work, bytes_accessed=2**20, transcendentals=0),
+        name="pulls",
     )(disp, mass, elem_nodes, elem_part.reshape(1, -1), elem_scale.reshape(1, -1), part_stiff)
 
     group = math.gcd(pairs, 8)
@@ -412,9 +436,11 @@
         in_specs=[VMEM, VMEM, VMEM, SMEM, SMEM, SMEM],
         out_specs=(VMEM, VMEM),
         scratch_shapes=[
+            pltpu.VMEM((blocks, 48, width), BF16),
             pltpu.VMEM((blocks, width, 48), BF16),
             pltpu.VMEM((blocks, 32, 2 * width), BF16),
             pltpu.VMEM((peers * cap, 48, width), BF16),
+            pltpu.VMEM((peers * cap, width, 48), BF16),
             pltpu.VMEM((peers * cap, 32, 2 * width), BF16),
             pltpu.VMEM((blocks, 8, width), F32),
             pltpu.VMEM((peers * cap, 8, width), F32),
@@ -424,6 +450,16 @@
         name="pairs",
     )(own, arrived, ratio, pair_a, pair_slot, pair_mask)
     returned = lax.all_to_all(going_back, axes, split_axis=0, concat_axis=0, tiled=True)
+
+    force = pl.pallas_call(
+        functools.partial(force_kernel, chunk),
+        out_shape=shape(3 * depth, WIDE),
+        in_specs=[VMEM, VMEM, pl.BlockSpec(memory_space=pl.ANY)],
+        out_specs=VMEM,
+        compiler_params=PARAMS,
+        cost_estimate=pl.CostEstimate(flops=12 * work, bytes_accessed=2**20, transcendentals=0),
+        name="forces",
+    )(pull, elem_nodes, seg_force)
 
     piece = math.gcd(share, 1024)
     total, lower, upper, time_step = pl.pallas_call(

time: 168 us -> 110 us (0.65)
  Pallas kernels: 130 us -> 78.1 us
  blocking collectives: 16.3 us -> 0 us
  starting transfers between devices: 11.5 us -> 17.4 us
  local copies, waits for them, and re-layouts: 4.89 us -> 8.83 us
    pallas_call x1, Pallas kernels: 95.4 us -> 42.4 us  [shards(): pl.pallas_call(functools.partial(pair_kernel, cap, group), out_shape=(sha...]
    all_to_all x1 -> x0, blocking collectives: 16.3 us -> none  [shards(): lax.all_to_all(going_back, axes, split_axis=0, concat_axis=0, tiled=True)]
    all_to_all x0 -> x1, starting transfers between devices: none -> 5.84 us  [shards(): lax.all_to_all(going_back, axes, split_axis=0, concat_axis=0, tiled=True)]
    pallas_call x1 -> x2, Pallas kernels: 24 us -> 21.8 us  [the longest x1 11.9 us: shards(): pl.pallas_call(functools.partial(pull_kernel, chunk), out_shape=(shape(12...]
    pallas_call x1, Pallas kernels: 1.07 us -> 2.81 us  [shards(): pl.pallas_call(functools.partial(update_kernel, piece), out_shape=(shape(...]
  transfers between devices with their start and end apart: 3 -> 4, of which waited for: 2 -> 2; matrix products, arithmetic and copies ran while one was open for 0% -> 1% of each run, Pallas kernels for 14% -> 20%
where the time goes in v2:
time: 110 us
  Pallas kernels  78.1 us (71%)
  starting transfers between devices  17.4 us (16%)
  local copies, waits for them, and re-layouts  8.83 us (8%)
  waiting for transfers between devices  4.71 us (4%)
    pallas_call x1, Pallas kernels, shards(): pl.pallas_call(functools.partial(pair_kernel, cap, group), out_shape=(sha...  42.4 us
    pallas_call x1, Pallas kernels, shards(): pl.pallas_call(functools.partial(pull_kernel, chunk), out_shape=(shape(12...  11.9 us
    pallas_call x1, Pallas kernels, shards(): pl.pallas_call(functools.partial(force_kernel, chunk), out_shape=shape(3...  9.93 us
    all_to_all x1, starting transfers between devices, shards(): lax.all_to_all(outgoing, axes, split_axis=0, concat_axis=0, tiled=True)  7.3 us
    pallas_call x1, Pallas kernels, shards(): pl.pallas_call(functools.partial(total_kernel, cap, piece), out_shape=(sh...  6.21 us
    all_to_all x1, starting transfers between devices, shards(): lax.all_to_all(going_back, axes, split_axis=0, concat_axis=0, tiled=True)  5.84 us
    pallas_call x1, Pallas kernels, shards(): pl.pallas_call(functools.partial(segment_kernel, cap), out_shape=(shape(b...  4.88 us
    ppermute x2, starting transfers between devices, shifted(): lax.ppermute(value, axis, [(source, source + steps) for source in range(f...  4.23 us
  transfers between devices with their start and end apart: 4, of which 2 were waited for; matrix products, arithmetic and copies ran while one was open for 1% of the time, Pallas kernels for 20%

profile of v2, /device:TPU:0, one launch (start us, length us, event | category | flops | bytes accessed | tf_op | source)
XLA Modules:
  0.0 109.8 jit_solution(13667243598202525412)
XLA Ops:
  0.6 0.0 copy-start.8
  0.6 0.0 copy-start.2
  0.6 1.7 %reshape.32.disp_ref = f32[96,256]{1,0:T(8,128)} reshape(f32[3,8192]{1,0:T(4,128)} %param.16) | data formatting | bytes 196608 | tf_op jit(solution)/shard_map/reshape | solution.py:406
  2.3 0.0 copy-done.8
  2.3 0.1 copy.17
  2.4 0.7 reshape.33.send_ref
  3.1 0.0 copy-done.2
  3.1 0.7 reshape.31.pos_ref
  3.8 4.9 %segments.1 = (f32[64,8,128]{2,1,0:T(8,128)}, f32[32,16,128]{2,1,0:T(8,128)}) custom-call(f32[96,256]{1,0:T(8,128)} %reshape.31.pos_ref, f32[96,256]{1,0:T(8,128)} %reshape.32.disp_ref, s32[64,128]{1,0:T(8,128)} %seg_ref.3, s32[64,128]{1,0:T(8,128)} %mask_ref.1, s32[160]{0:T(256)} %reshape.33.send_ref), custom_call_target="tpu_custom_call" | custom-call | tf_op jit(solution)/shard_map/segments/pallas_call | solution.py:410
  8.7 0.0 copy-start.7
  8.7 7.3 %all-to-all-start = ((f32[32,16,128]{2,1,0:T(8,128)}), f32[32,16,128]{2,1,0:T(8,128)S(1)}, u32[]{:S(2)}, u32[]{:S(2)}) async-start(f32[32,16,128]{2,1,0:T(8,128)} %get-tuple-element.15), calls=%async_computation | async-start | bytes 524288 | tf_op jit(solution)/shard_map/all_to_all | solution.py:418
  16.0 0.0 copy-done.7
  16.0 0.6 reshape.34.mass_ref
  16.6 11.9 %pulls.1 = (f32[12,8192]{1,0:T(8,128)}, f32[8,128]{1,0:T(8,128)}) custom-call(f32[96,256]{1,0:T(8,128)} %reshape.32.disp_ref, f32[32,256]{1,0:T(8,128)} %reshape.34.mass_ref, s32[4,8192]{1,0:T(4,128)} %nodes_ref.3, s32[1,8192]{1,0:T(1,128)} %bitcast.2, f32[1,8192]{1,0:T(1,128)} %bitcast.3, f32[4]{0:T(128)} %stiff_ref.1), custom_call_target="tpu_custom_call" | custom-call | flops 6442450944 | bytes 1048576 | tf_op jit(solution)/shard_map/pulls/pallas_call | solution.py:422
  28.5 0.0 all-to-all-done.got_ref
  28.5 0.0 copy-start.1
  28.5 0.7 copy-done.1
  29.2 42.4 %pairs.1 = (f32[64,8,128]{2,1,0:T(8,128)}, f32[32,16,128]{2,1,0:T(8,128)}) custom-call(f32[64,8,128]{2,1,0:T(8,128)} %get-tuple-element.14.own_ref, f32[32,16,128]{2,1,0:T(8,128)} %copy-done.1, f32[8,128]{1,0:T(8,128)} %get-tuple-element.16.ratio_ref, s32[512]{0:T(512)} %first_ref.1, s32[512]{0:T(512)} %second_ref.1, s32[512]{0:T(512)} %live_ref.1), custom_call_target="tpu_custom_call" | custom-call | tf_op jit(solution)/shard_map/pairs/pallas_call | solution.py:433
  71.6 5.8 %all-to-all-start.1 = ((f32[32,16,128]{2,1,0:T(8,128)}), f32[32,16,128]{2,1,0:T(8,128)S(1)}, u32[]{:S(2)}, u32[]{:S(2)}) async-start(f32[32,16,128]{2,1,0:T(8,128)} %get-tuple-element.17), calls=%async_computation.1 | async-start | bytes 524288 | tf_op jit(solution)/shard_map/all_to_all | solution.py:452
  77.5 9.9 %forces.1.force_ref = f32[96,256]{1,0:T(8,128)} custom-call(f32[12,8192]{1,0:T(8,128)} %get-tuple-element.19.pull_ref, s32[4,8192]{1,0:T(4,128)} %nodes_ref.3, f32[64,8,128]{2,1,0:T(8,128)} %get-tuple-element.18.after_ref.own_ref), custom_call_target="tpu_custom_call" | custom-call | flops 6442450944 | bytes 1048576 | tf_op jit(solution)/shard_map/forces/pallas_call | solution.py:454
  87.4 0.0 copy-start.3
  87.4 0.7 all-to-all-done.1.back_ref
  88.1 0.0 copy-start
  88.1 0.7 copy-done
  88.8 6.2 %totals.1 = (f32[96,256]{1,0:T(8,128)}, f32[3,2048]{1,0:T(4,128)}, f32[3,2048]{1,0:T(4,128)}, f32[8,128]{1,0:T(8,128)}) custom-call(f32[32,16,128]{2,1,0:T(8,128)} %copy-done, s32[160]{0:T(256)} %reshape.33.send_ref, f32[64,8,128]{2,1,0:T(8,128)} %get-tuple-element.18.after_ref.own_ref, s32[64,128]{1,0:T(8,128)} %seg_ref.3, f32[96,256]{1,0:T(8,128)} %forces.1.force_ref, ...), custom_call_target="tpu_custom_call" | custom-call | tf_op jit(solution)/shard_map/totals/pallas_call | solution.py:465
  95.0 2.9 %collective-permute-start = (f32[3,2048]{1,0:T(4,128)}, f32[3,2048]{1,0:T(4,128)S(1)}, u32[]{:S(2)}, u32[]{:S(2)}) collective-permute-start(f32[3,2048]{1,0:T(4,128)} %get-tuple-element.21), channel_id=1, source_target_pairs={{0,1},{1,2},{2,3},{3,4},{4,5},{5,6},{6,7},{8,9},{9,10},{10,11},{11... | collective-permute-start | bytes 73736 | tf_op jit(solution)/shard_map/ppermute | solution.py:27
  98.0 1.3 %collective-permute-start.1 = (f32[3,2048]{1,0:T(4,128)}, f32[3,2048]{1,0:T(4,128)S(1)}, u32[]{:S(2)}, u32[]{:S(2)}) collective-permute-start(f32[3,2048]{1,0:T(4,128)} %get-tuple-element.22), channel_id=1, source_target_pairs={{1,0},{2,1},{3,2},{4,3},{5,4},{6,5},{7,6},{9,8},{10,9},{11,10},{12... | collective-permute-start | bytes 73736 | tf_op jit(solution)/shard_map/ppermute | solution.py:27
  99.3 0.0 copy-done.3
  99.3 0.7 reshape.37.vel_ref
  100.0 0.0 collective-permute-done.lower_ref
  100.0 0.0 copy-start.5
  100.0 4.0 %collective-permute-done.1.upper_ref = f32[3,2048]{1,0:T(4,128)S(1)} collective-permute-done((f32[3,2048]{1,0:T(4,128)}, f32[3,2048]{1,0:T(4,128)S(1)}, u32[]{:S(2)}, u32[]{:S(2)}) %collective-permute-start.1) | collective-permute-done | bytes 24608 | tf_op jit(solution)/shard_map/ppermute | solution.py:27
  104.0 0.0 copy-start.6
  104.0 0.0 copy-done.5
  104.0 0.6 copy-done.6
  104.6 2.8 %update.1 = (f32[96,256]{1,0:T(8,128)}, f32[96,256]{1,0:T(8,128)}) custom-call(f32[96,256]{1,0:T(8,128)} %get-tuple-element.20.total_ref, f32[3,2048]{1,0:T(4,128)} %copy-done.5, f32[3,2048]{1,0:T(4,128)} %copy-done.6, s32[2,2048]{1,0:T(2,128)} %shared_ref.3, f32[32,256]{1,0:T(8,128)} %reshape.34.mass_ref, f32[96,256]{1,0:T(8,128)} %reshape.37.vel_ref, ...), custom_call_target="tpu_custom_call" | custom-call | tf_op jit(solution)/shard_map/update/pallas_call | solution.py:477
  107.4 0.0 copy-start.4
  107.4 1.6 %reshape.38 = f32[3,8192]{1,0:T(4,128)} reshape(f32[96,256]{1,0:T(8,128)} %get-tuple-element.24) | data formatting | bytes 196608 | tf_op jit(solution)/shard_map/reshape | solution.py:485
  109.1 0.0 copy-done.4
  109.1 0.7 reshape.39
Async XLA Ops:
  0.6 1.7 %copy-start.8 = (s32[1,32,5]{1,0,2:T(1,128)S(1)}, s32[1,32,5]{1,0,2:T(1,128)}, u32[]{:S(2)}) copy-start(s32[1,32,5]{1,0,2:T(1,128)} %param.26) | copy-start | bytes 1924
  0.6 2.4 %copy-start.2 = (f32[3,8192]{1,0:T(4,128)S(1)}, f32[3,8192]{1,0:T(4,128)}, u32[]{:S(2)}) copy-start(f32[3,8192]{1,0:T(4,128)} %param.15) | copy-start | bytes 294916
  8.7 7.3 %copy-start.7 = (f32[8192]{0:T(1024)S(1)}, f32[8192]{0:T(1024)}, u32[]{:S(2)}) copy-start(f32[8192]{0:T(1024)} %param.18) | copy-start | bytes 98308
  8.7 19.8 %all-to-all-start = ((f32[32,16,128]{2,1,0:T(8,128)}), f32[32,16,128]{2,1,0:T(8,128)S(1)}, u32[]{:S(2)}, u32[]{:S(2)}) async-start(f32[32,16,128]{2,1,0:T(8,128)} %get-tuple-element.15), calls=%async_computation | async-start | bytes 524288 | tf_op jit(solution)/shard_map/all_to_all | solution.py:418
  28.5 0.7 copy-start.1
  71.6 16.5 %all-to-all-start.1 = ((f32[32,16,128]{2,1,0:T(8,128)}), f32[32,16,128]{2,1,0:T(8,128)S(1)}, u32[]{:S(2)}, u32[]{:S(2)}) async-start(f32[32,16,128]{2,1,0:T(8,128)} %get-tuple-element.17), calls=%async_computation.1 | async-start | bytes 524288 | tf_op jit(solution)/shard_map/all_to_all | solution.py:452
  87.4 11.9 %copy-start.3 = (f32[3,8192]{1,0:T(4,128)S(1)}, f32[3,8192]{1,0:T(4,128)}, u32[]{:S(2)}) copy-start(f32[3,8192]{1,0:T(4,128)} %param.17) | copy-start | bytes 294916
  88.1 0.7 copy-start
  95.0 5.0 %collective-permute-start = (f32[3,2048]{1,0:T(4,128)}, f32[3,2048]{1,0:T(4,128)S(1)}, u32[]{:S(2)}, u32[]{:S(2)}) collective-permute-start(f32[3,2048]{1,0:T(4,128)} %get-tuple-element.21), channel_id=1, source_target_pairs={{0,1},{1,2},{2,3},{3,4},{4,5},{5,6},{6,7},{8,9},{9,10},{10,11},{11... | collective-permute-start | bytes 73736 | tf_op jit(solution)/shard_map/ppermute | solution.py:27
  98.0 6.0 %collective-permute-start.1 = (f32[3,2048]{1,0:T(4,128)}, f32[3,2048]{1,0:T(4,128)S(1)}, u32[]{:S(2)}, u32[]{:S(2)}) collective-permute-start(f32[3,2048]{1,0:T(4,128)} %get-tuple-element.22), channel_id=1, source_target_pairs={{1,0},{2,1},{3,2},{4,3},{5,4},{6,5},{7,6},{9,8},{10,9},{11,10},{12... | collective-permute-start | bytes 73736 | tf_op jit(solution)/shard_map/ppermute | solution.py:27
  100.0 4.0 %copy-start.5 = (f32[3,2048]{1,0:T(4,128)}, f32[3,2048]{1,0:T(4,128)S(1)}, u32[]{:S(2)}) copy-start(f32[3,2048]{1,0:T(4,128)S(1)} %collective-permute-done.lower_ref) | copy-start | bytes 73732
  104.0 0.6 copy-start.6
  107.4 1.6 %copy-start.4 = (f32[96,256]{1,0:T(8,128)S(1)}, f32[96,256]{1,0:T(8,128)}, u32[]{:S(2)}) copy-start(f32[96,256]{1,0:T(8,128)} %get-tuple-element.25) | copy-start | bytes 294916

commit v3 on v2

--- a/solution.py
+++ b/solution.py
@@ -71,15 +71,37 @@
     return sums[:half] + sums[half:]
 
 
+def fold(ref, to_ref, first=0):
+    rows, nodes = ref.shape
+    depth = nodes // WIDE
+    for row in range(rows):
+        for high in range(depth):
+            place = first + row * depth + high
+            to_ref[place : place + 1, :] = ref[row : row + 1, high * WIDE : (high + 1) * WIDE]
+
+
+def unfold(ref, to_ref):
+    rows, nodes = to_ref.shape
+    depth = nodes // WIDE
+    for row in range(rows):
+        for high in range(depth):
+            place = row * depth + high
+            to_ref[row : row + 1, high * WIDE : (high + 1) * WIDE] = ref[place : place + 1, :]
+
+
 def lane_row(ref, start, count):
     tile = ref[pl.ds(pl.multiple_of(start, 8), count), :]
     return jnp.concatenate([tile[row : row + 1] for row in range(count)], 1)
 
 
-def segment_kernel(cap, pos_ref, disp_ref, seg_ref, mask_ref, send_ref, own_ref, out_ref):
-    depth = pos_ref.shape[0] // 3
+def segment_kernel(
+    cap, pos_ref, disp_ref, seg_ref, mask_ref, send_ref, own_ref, out_ref, table_ref, moved_ref
+):
+    depth = table_ref.shape[0] // 3
     blocks, width = seg_ref.shape
-    table = split_table(pos_ref[...] + disp_ref[...])
+    moved_ref[...] = pos_ref[...] + disp_ref[...]
+    fold(moved_ref, table_ref)
+    table = split_table(table_ref[...])
 
     def gather(step, carry):
         start = step * 8
@@ -99,7 +121,7 @@
 
     def send(peer, carry):
         for slot in range(cap):
-            block = own_ref[send_ref[peer * cap + slot], 0:3, :]
+            block = own_ref[send_ref[0, peer, slot], 0:3, :]
             out_ref[peer, 3 * slot : 3 * slot + 3, :] = jnp.where(
                 block < -0.5 * FAR_AWAY, FAR_AWAY, block
             )
@@ -110,12 +132,14 @@
 
 
 def pull_kernel(
-    chunk, disp_ref, mass_ref, nodes_ref, part_ref, scale_ref, stiff_ref, pull_ref, ratio_ref
+    chunk, disp_ref, mass_ref, nodes_ref, part_ref, scale_ref, stiff_ref, pull_ref, ratio_ref, table_ref
 ):
-    depth = mass_ref.shape[0]
+    depth = table_ref.shape[0] // 4
     elems = nodes_ref.shape[1]
     parts = stiff_ref.shape[0]
-    table = split_table(jnp.concatenate([disp_ref[...], mass_ref[...]], 0))
+    fold(disp_ref, table_ref)
+    fold(mass_ref, table_ref, 3 * depth)
+    table = split_table(table_ref[...])
 
     def one_chunk(step, best):
         lanes = pl.ds(pl.multiple_of(step * chunk, chunk), chunk)
@@ -192,24 +216,31 @@
     pairs = first_ref.shape[0]
     scale = 2.0 * LOG2E
 
-    def doubled(parts):
-        stacked = jnp.concatenate(parts + [jnp.zeros_like(parts[0])], 0)
-        return jnp.concatenate([stacked, stacked], 1).astype(BF16)
+    row_id = lax.broadcasted_iota(jnp.int32, (8, width), 0)
+    pad = jnp.zeros((16, width), BF16)
+    gap = jnp.zeros((64, width), BF16)
+
+    def operands(tile):
+        one, two, three = split3(tile)
+        mixed = jnp.where(row_id < 3, two, pltpu.roll(three, 3, 0))
+        mixed = jnp.where(row_id < 6, mixed, 0.0)
+        columns = jnp.concatenate([one, mixed], 0)
+        return one, two, three, jnp.concatenate([columns, columns], 1).astype(BF16)
 
     def prepare_near(step, carry):
         for member in range(8):
             block = 8 * step + member
-            one, two, three = split3(own_ref[block])
-            rows = jnp.concatenate([one, one, two, two, one, three], 0)
-            near_rows[block] = rows.astype(BF16)
-            near_turn[block] = rows.T.astype(BF16)
-            near_cols[block] = doubled([one, two, three])
-            near_sum[block] = jnp.zeros((8, width), F32)
+            one, two, three, columns = operands(own_ref[block])
+            rows = jnp.concatenate([one, one, two, two, one, three], 0).astype(BF16)
+            rows = jnp.concatenate([rows, pad], 0)
+            near_rows[block] = rows
+            near_turn[block] = jnp.concatenate([rows, gap], 0).T
+            near_cols[block] = columns
+            near_sum[block] = jnp.zeros((16, width), F32)
         return carry
 
     lax.fori_loop(0, blocks // 8, prepare_near, 0)
 
-    row_id = lax.broadcasted_iota(jnp.int32, (8, width), 0)
     tile_ref[...] = jnp.zeros_like(tile_ref)
 
     def prepare_far(peer, carry):
@@ -218,24 +249,19 @@
         for slot in range(cap):
             tile = tile_ref[slot]
             square = -LOG2E * jnp.sum(tile * tile, 0, keepdims=True)
-            one, two, three = split3(
+            one, two, three, columns = operands(
                 jnp.where(row_id == 3, square, jnp.where(row_id == 4, 1.0, scale * tile))
             )
             place = peer * cap + slot
-            rows = jnp.concatenate([one, two, one, two, three, one], 0)
-            far_rows[place] = rows.astype(BF16)
-            far_turn[place] = rows.T.astype(BF16)
-            far_cols[place] = doubled([one, two, three])
-            far_sum[place] = jnp.zeros((8, width), F32)
+            rows = jnp.concatenate([one, two, one, two, three, one], 0).astype(BF16)
+            rows = jnp.concatenate([rows, pad], 0)
+            far_rows[place] = rows
+            far_turn[place] = jnp.concatenate([gap, rows], 0).T
+            far_cols[place] = columns
+            far_sum[place] = jnp.zeros((16, width), F32)
         return carry
 
     lax.fori_loop(0, peers, prepare_far, 0)
-
-    def weights(left, right):
-        weight = jnp.exp2(jnp.dot(left, right, preferred_element_type=F32))
-        first = weight.astype(BF16)
-        second = (weight - first.astype(F32)).astype(BF16)
-        return jnp.concatenate([first, second], 0)
 
     def one_group(step, carry):
         results = []
@@ -243,15 +269,25 @@
             place = step * group + member
             near, far = first_ref[place], second_ref[place]
             live = live_ref[place].astype(F32)
-            pushed = jnp.dot(
-                far_cols[far], weights(far_turn[far], near_rows[near]), preferred_element_type=F32
+            right = jnp.concatenate(
+                [
+                    jnp.concatenate([far_rows[far], gap], 1),
+                    jnp.concatenate([gap, near_rows[near]], 1),
+                ],
+                0,
             )
-            recoil = jnp.dot(
-                near_cols[near], weights(near_turn[near], far_rows[far]), preferred_element_type=F32
+            both = jnp.dot(
+                near_turn[near] + far_turn[far], right, preferred_element_type=F32
             )
-            pushed = live * (pushed[0:8] + pushed[8:16] + pushed[16:24])
-            recoil = live * (recoil[0:8] + recoil[8:16] + recoil[16:24])
-            results.append((near, far, pushed, recoil))
+            weight = jnp.exp2(both)
+            first = weight.astype(BF16)
+            second = (weight - first.astype(F32)).astype(BF16)
+            sums = jnp.dot(
+                jnp.concatenate([near_cols[near], far_cols[far]], 0),
+                jnp.concatenate([first, second], 0),
+                preferred_element_type=F32,
+            )
+            results.append((near, far, live * sums[16:, width:], live * sums[:16, :width]))
         for near, far, pushed, recoil in results:
             near_sum[near] += pushed
             far_sum[far] += recoil
@@ -259,10 +295,14 @@
 
     lax.fori_loop(0, pairs // group, one_group, 0)
 
+    def joined(sums):
+        low = sums[8:16]
+        return sums[:8] + jnp.where(row_id < 3, low + pltpu.roll(low, 5, 0), 0.0)
+
     def finish_near(step, carry):
         for member in range(8):
             block = 8 * step + member
-            sums = near_sum[block]
+            sums = joined(near_sum[block])
             seg_ref[block] = own_ref[block] * sums[4:5] - (1.0 / scale) * sums
         return carry
 
@@ -271,7 +311,7 @@
     def finish_far(peer, carry):
         for slot in range(cap):
             rows = slice(3 * slot, 3 * slot + 3)
-            sums = far_sum[peer * cap + slot]
+            sums = joined(far_sum[peer * cap + slot])
             back_ref[peer, rows, :] = got_ref[peer, rows, :] * sums[3:4] - sums[0:3]
         back_ref[peer, 3 * cap :, :] = jnp.broadcast_to(
             ratio_ref[0:1], (back_ref.shape[1] - 3 * cap, width)
@@ -302,7 +342,7 @@
 
     def give_back(peer, best):
         for slot in range(cap):
-            block = send_ref[peer * cap + slot]
+            block = send_ref[0, peer, slot]
             sums[block, 0:3, :] += back_ref[peer, 3 * slot : 3 * slot + 3, :]
         return jnp.minimum(best, back_ref[peer, 3 * cap : 3 * cap + 1, :])
 
@@ -350,26 +390,25 @@
     step_ref,
     new_disp_ref,
     new_vel_ref,
+    sums,
 ):
-    depth = mass_ref.shape[0]
-    new_vel_ref[...] = total_ref[...]
+    sums[...] = total_ref[...]
+    depth = sums.shape[0] // 3
 
     def scatter(step, carry):
         lanes = pl.ds(pl.multiple_of(step * chunk, chunk), chunk)
         for side, in_ref in ((0, lower_ref), (1, upper_ref)):
             hot, mask = selectors(shared_ref[side : side + 1, lanes], depth)
             rows = [in_ref[row : row + 1, lanes] for row in range(3)]
-            new_vel_ref[...] += spread(rows, hot, mask)
+            sums[...] += spread(rows, hot, mask)
         return carry
 
     lax.fori_loop(0, shared_ref.shape[1] // chunk, scatter, 0)
+    unfold(sums, new_vel_ref)
     time_step = step_ref[0:1, 0:1]
-    mass = mass_ref[...]
-    for axis in range(3):
-        rows = slice(axis * depth, (axis + 1) * depth)
-        velocity = vel_ref[rows, :] + time_step * (new_vel_ref[rows, :] / mass)
-        new_vel_ref[rows, :] = velocity
-        new_disp_ref[rows, :] = disp_ref[rows, :] + time_step * velocity
+    velocity = vel_ref[...] + time_step * (new_vel_ref[...] / mass_ref[...])
+    new_vel_ref[...] = velocity
+    new_disp_ref[...] = disp_ref[...] + time_step * velocity
 
 
 def shape(*dims):
@@ -402,19 +441,17 @@
     share = shared.shape[1]
     depth = nodes // WIDE
     slab = -(-(3 * cap + 1) // 8) * 8
-    pos = ref_pos.reshape(3 * depth, WIDE)
-    disp = displacement.reshape(3 * depth, WIDE)
-    mass = node_mass.reshape(depth, WIDE)
-    send = send_blk.reshape(-1)
+    mass = node_mass.reshape(1, -1)
 
     own, outgoing = pl.pallas_call(
         functools.partial(segment_kernel, cap),
         out_shape=(shape(blocks, 8, width), shape(peers, slab, width)),
         in_specs=[VMEM, VMEM, VMEM, VMEM, SMEM],
         out_specs=(VMEM, VMEM),
+        scratch_shapes=[pltpu.VMEM((3 * depth, WIDE), F32), pltpu.VMEM((3, nodes), F32)],
         compiler_params=PARAMS,
         name="segments",
-    )(pos, disp, seg_node, seg_mask, send)
+    )(ref_pos, displacement, seg_node, seg_mask, send_blk)
     arrived = lax.all_to_all(outgoing, axes, split_axis=0, concat_axis=0, tiled=True)
 
     chunk = math.gcd(elems, 512)
@@ -424,10 +461,11 @@
         out_shape=(shape(12, elems), shape(8, width)),
         in_specs=[VMEM, VMEM, VMEM, VMEM, VMEM, SMEM],
         out_specs=(VMEM, VMEM),
+        scratch_shapes=[pltpu.VMEM((4 * depth, WIDE), F32)],
         compiler_params=PARAMS,
         cost_estimate=pl.CostEstimate(flops=12 * work, bytes_accessed=2**20, transcendentals=0),
         name="pulls",
-    )(disp, mass, elem_nodes, elem_part.reshape(1, -1), elem_scale.reshape(1, -1), part_stiff)
+    )(displacement, mass, elem_nodes, elem_part.reshape(1, -1), elem_scale.reshape(1, -1), part_stiff)
 
     group = math.gcd(pairs, 8)
     seg_force, going_back = pl.pallas_call(
@@ -436,14 +474,14 @@
         in_specs=[VMEM, VMEM, VMEM, SMEM, SMEM, SMEM],
         out_specs=(VMEM, VMEM),
         scratch_shapes=[
-            pltpu.VMEM((blocks, 48, width), BF16),
-            pltpu.VMEM((blocks, width, 48), BF16),
-            pltpu.VMEM((blocks, 32, 2 * width), BF16),
-            pltpu.VMEM((peers * cap, 48, width), BF16),
-            pltpu.VMEM((peers * cap, width, 48), BF16),
-            pltpu.VMEM((peers * cap, 32, 2 * width), BF16),
-            pltpu.VMEM((blocks, 8, width), F32),
-            pltpu.VMEM((peers * cap, 8, width), F32),
+            pltpu.VMEM((blocks, 64, width), BF16),
+            pltpu.VMEM((blocks, width, width), BF16),
+            pltpu.VMEM((blocks, 16, 2 * width), BF16),
+            pltpu.VMEM((peers * cap, 64, width), BF16),
+            pltpu.VMEM((peers * cap, width, width), BF16),
+            pltpu.VMEM((peers * cap, 16, 2 * width), BF16),
+            pltpu.VMEM((blocks, 16, width), F32),
+            pltpu.VMEM((peers * cap, 16, width), F32),
             pltpu.VMEM((cap, 8, width), F32),
         ],
         compiler_params=PARAMS,
@@ -470,19 +508,19 @@
         scratch_shapes=[pltpu.VMEM((blocks, 8, width), F32)],
         compiler_params=PARAMS,
         name="totals",
-    )(returned, send, seg_force, seg_node, force, shared)
+    )(returned, send_blk, seg_force, seg_node, force, shared)
     from_lower = shifted(lower, "dev", 1)
     from_upper = shifted(upper, "dev", -1)
 
-    new_disp, new_vel = pl.pallas_call(
+    return pl.pallas_call(
         functools.partial(update_kernel, piece),
-        out_shape=(shape(3 * depth, WIDE), shape(3 * depth, WIDE)),
+        out_shape=(shape(3, nodes), shape(3, nodes)),
         in_specs=[VMEM] * 8,
         out_specs=(VMEM, VMEM),
+        scratch_shapes=[pltpu.VMEM((3 * depth, WIDE), F32)],
         compiler_params=PARAMS,
         name="update",
-    )(total, from_lower, from_upper, shared, mass, velocity.reshape(3 * depth, WIDE), disp, time_step)
-    return (new_disp.reshape(3, nodes), new_vel.reshape(3, nodes))
+    )(total, from_lower, from_upper, shared, mass, velocity, displacement, time_step)
 
 
 def solution(mesh):

time: 110 us -> 106 us (0.964)
  local copies, waits for them, and re-layouts: 8.83 us -> 3.36 us
    reshape x7 -> x0, local copies, waits for them, and re-layouts: 6.72 us -> none  [the longest x2 2.35 us: shards(): return (new_disp.reshape(3, nodes), new_vel.reshape(3, nodes))]
    unnamed x19 -> x9, local copies, waits for them, and re-layouts: 2.11 us -> 3.36 us
  transfers between devices with their start and end apart: 4 -> 4, of which waited for: 2 -> 3; matrix products, arithmetic and copies ran while one was open for 1% -> 0% of each run, Pallas kernels for 20% -> 21%
where the time goes in v3:
time: 106 us; the launch traced here: 105 us
  Pallas kernels  78.3 us (74%)
  starting transfers between devices  17.4 us (16%)
  waiting for transfers between devices  5.5 us (5%)
  local copies, waits for them, and re-layouts  3.36 us (3%)
    pallas_call x1, Pallas kernels, shards(): pl.pallas_call(functools.partial(pair_kernel, cap, group), out_shape=(sha...  42.5 us
    pallas_call x1, Pallas kernels, shards(): pl.pallas_call(functools.partial(pull_kernel, chunk), out_shape=(shape(12...  11.9 us
    pallas_call x1, Pallas kernels, shards(): pl.pallas_call(functools.partial(force_kernel, chunk), out_shape=shape(3...  9.86 us
    all_to_all x1, starting transfers between devices, shards(): lax.all_to_all(outgoing, axes, split_axis=0, concat_axis=0, tiled=True)  7.3 us
    pallas_call x1, Pallas kernels, shards(): pl.pallas_call(functools.partial(total_kernel, cap, piece), out_shape=(sh...  6.19 us
    all_to_all x1, starting transfers between devices, shards(): lax.all_to_all(going_back, axes, split_axis=0, concat_axis=0, tiled=True)  5.83 us
    pallas_call x1, Pallas kernels, shards(): pl.pallas_call(functools.partial(segment_kernel, cap), out_shape=(shape(b...  5.02 us
    ppermute x2, waiting for transfers between devices, shifted(): lax.ppermute(value, axis, [(source, source + steps) for source in range(f...  4.72 us
  transfers between devices with their start and end apart: 4, of which 3 were waited for; matrix products, arithmetic and copies ran while one was open for 0% of the time, Pallas kernels for 21%

profile of v3, /device:TPU:0, one launch (start us, length us, event | category | flops | bytes accessed | tf_op | source)
XLA Modules:
  0.0 105.2 jit_solution(17252364967314931955)
XLA Ops:
  0.6 1.4 %copy.17.send_ref = s32[1,32,5]{2,1,0:T(8,128)} copy(s32[1,32,5]{1,0,2:T(1,128)} %param.26) | data formatting | bytes 1280 | tf_op args[11]
  2.0 5.0 %segments.1 = (f32[64,8,128]{2,1,0:T(8,128)}, f32[32,16,128]{2,1,0:T(8,128)}) custom-call(f32[3,8192]{1,0:T(4,128)} %pos_ref.1, f32[3,8192]{1,0:T(4,128)} %disp_ref.5, s32[64,128]{1,0:T(8,128)} %seg_ref.3, s32[64,128]{1,0:T(8,128)} %mask_ref.1, s32[1,32,5]{2,1,0:T(8,128)} %copy.17.send_ref), custom_call_target="tpu_custom_call" | custom-call | tf_op jit(solution)/shard_map/segments/pallas_call | solution.py:446
  7.0 7.3 %all-to-all-start = ((f32[32,16,128]{2,1,0:T(8,128)}), f32[32,16,128]{2,1,0:T(8,128)S(1)}, u32[]{:S(2)}, u32[]{:S(2)}) async-start(f32[32,16,128]{2,1,0:T(8,128)} %get-tuple-element.13), calls=%async_computation | async-start | bytes 524288 | tf_op jit(solution)/shard_map/all_to_all | solution.py:455
  14.3 11.9 %pulls.1 = (f32[12,8192]{1,0:T(8,128)}, f32[8,128]{1,0:T(8,128)}) custom-call(f32[3,8192]{1,0:T(4,128)} %disp_ref.5, f32[1,8192]{1,0:T(1,128)} %bitcast.3, s32[4,8192]{1,0:T(4,128)} %nodes_ref.3, s32[1,8192]{1,0:T(1,128)} %bitcast.5, f32[1,8192]{1,0:T(1,128)} %bitcast.6, f32[4]{0:T(128)} %stiff_ref.1), custom_call_target="tpu_custom_call" | custom-call | flops 6442450944 | bytes 1048576 | tf_op jit(solution)/shard_map/pulls/pallas_call | solution.py:459
  26.2 0.0 all-to-all-done.got_ref
  26.2 0.0 copy-start.1
  26.2 0.7 copy-done.1
  26.9 42.5 %pairs.1 = (f32[64,8,128]{2,1,0:T(8,128)}, f32[32,16,128]{2,1,0:T(8,128)}) custom-call(f32[64,8,128]{2,1,0:T(8,128)} %get-tuple-element.12.own_ref, f32[32,16,128]{2,1,0:T(8,128)} %copy-done.1, f32[8,128]{1,0:T(8,128)} %get-tuple-element.14.ratio_ref, s32[512]{0:T(512)} %first_ref.1, s32[512]{0:T(512)} %second_ref.1, s32[512]{0:T(512)} %live_ref.1), custom_call_target="tpu_custom_call" | custom-call | tf_op jit(solution)/shard_map/pairs/pallas_call | solution.py:471
  69.4 5.8 %all-to-all-start.1 = ((f32[32,16,128]{2,1,0:T(8,128)}), f32[32,16,128]{2,1,0:T(8,128)S(1)}, u32[]{:S(2)}, u32[]{:S(2)}) async-start(f32[32,16,128]{2,1,0:T(8,128)} %get-tuple-element.15), calls=%async_computation.1 | async-start | bytes 524288 | tf_op jit(solution)/shard_map/all_to_all | solution.py:490
  75.2 9.9 %forces.1.force_ref = f32[96,256]{1,0:T(8,128)} custom-call(f32[12,8192]{1,0:T(8,128)} %get-tuple-element.17.pull_ref, s32[4,8192]{1,0:T(4,128)} %nodes_ref.3, f32[64,8,128]{2,1,0:T(8,128)} %get-tuple-element.16.after_ref.own_ref), custom_call_target="tpu_custom_call" | custom-call | flops 6442450944 | bytes 1048576 | tf_op jit(solution)/shard_map/forces/pallas_call | solution.py:492
  85.1 0.8 all-to-all-done.1.back_ref
  85.9 0.0 copy-start
  85.9 0.7 copy-done
  86.6 6.2 %totals.1 = (f32[96,256]{1,0:T(8,128)}, f32[3,2048]{1,0:T(4,128)}, f32[3,2048]{1,0:T(4,128)}, f32[8,128]{1,0:T(8,128)}) custom-call(f32[32,16,128]{2,1,0:T(8,128)} %copy-done, s32[1,32,5]{2,1,0:T(8,128)} %copy.17.send_ref, f32[64,8,128]{2,1,0:T(8,128)} %get-tuple-element.16.after_ref.own_ref, s32[64,128]{1,0:T(8,128)} %seg_ref.3, ...), custom_call_target="tpu_custom_call" | custom-call | tf_op jit(solution)/shard_map/totals/pallas_call | solution.py:503
  92.7 2.9 %collective-permute-start = (f32[3,2048]{1,0:T(4,128)}, f32[3,2048]{1,0:T(4,128)S(1)}, u32[]{:S(2)}, u32[]{:S(2)}) collective-permute-start(f32[3,2048]{1,0:T(4,128)} %get-tuple-element.19), channel_id=1, source_target_pairs={{0,1},{1,2},{2,3},{3,4},{4,5},{5,6},{6,7},{8,9},{9,10},{10,11},{11... | collective-permute-start | bytes 73736 | tf_op jit(solution)/shard_map/ppermute | solution.py:27
  95.7 1.3 %collective-permute-start.1 = (f32[3,2048]{1,0:T(4,128)}, f32[3,2048]{1,0:T(4,128)S(1)}, u32[]{:S(2)}, u32[]{:S(2)}) collective-permute-start(f32[3,2048]{1,0:T(4,128)} %get-tuple-element.20), channel_id=1, source_target_pairs={{1,0},{2,1},{3,2},{4,3},{5,4},{6,5},{7,6},{9,8},{10,9},{11,10},{12... | collective-permute-start | bytes 73736 | tf_op jit(solution)/shard_map/ppermute | solution.py:27
  97.0 0.6 collective-permute-done.lower_ref
  97.6 0.0 copy-start.2
  97.6 4.1 %collective-permute-done.1.upper_ref = f32[3,2048]{1,0:T(4,128)S(1)} collective-permute-done((f32[3,2048]{1,0:T(4,128)}, f32[3,2048]{1,0:T(4,128)S(1)}, u32[]{:S(2)}, u32[]{:S(2)}) %collective-permute-start.1) | collective-permute-done | bytes 24608 | tf_op jit(solution)/shard_map/ppermute | solution.py:27
  101.7 0.0 copy-start.3
  101.7 0.0 copy-done.2
  101.7 0.6 copy-done.3
  102.3 2.9 %update.1 = (f32[3,8192]{1,0:T(4,128)}, f32[3,8192]{1,0:T(4,128)}) custom-call(f32[96,256]{1,0:T(8,128)} %get-tuple-element.18.total_ref, f32[3,2048]{1,0:T(4,128)} %copy-done.2, f32[3,2048]{1,0:T(4,128)} %copy-done.3, s32[2,2048]{1,0:T(2,128)} %shared_ref.3, f32[1,8192]{1,0:T(1,128)} %bitcast.4, f32[3,8192]{1,0:T(4,128)} %vel_ref.1, f32[3,8192]{1,0:T(4,128)} %disp_ref.5, ...), custom_call_target="tpu_custom_call" | custom-call | tf_op jit(solution)/shard_map/update/pallas_call | solution.py:515
Async XLA Ops:
  7.0 19.2 %all-to-all-start = ((f32[32,16,128]{2,1,0:T(8,128)}), f32[32,16,128]{2,1,0:T(8,128)S(1)}, u32[]{:S(2)}, u32[]{:S(2)}) async-start(f32[32,16,128]{2,1,0:T(8,128)} %get-tuple-element.13), calls=%async_computation | async-start | bytes 524288 | tf_op jit(solution)/shard_map/all_to_all | solution.py:455
  26.2 0.7 copy-start.1
  69.4 16.5 %all-to-all-start.1 = ((f32[32,16,128]{2,1,0:T(8,128)}), f32[32,16,128]{2,1,0:T(8,128)S(1)}, u32[]{:S(2)}, u32[]{:S(2)}) async-start(f32[32,16,128]{2,1,0:T(8,128)} %get-tuple-element.15), calls=%async_computation.1 | async-start | bytes 524288 | tf_op jit(solution)/shard_map/all_to_all | solution.py:490
  85.9 0.7 copy-start
  92.7 4.8 %collective-permute-start = (f32[3,2048]{1,0:T(4,128)}, f32[3,2048]{1,0:T(4,128)S(1)}, u32[]{:S(2)}, u32[]{:S(2)}) collective-permute-start(f32[3,2048]{1,0:T(4,128)} %get-tuple-element.19), channel_id=1, source_target_pairs={{0,1},{1,2},{2,3},{3,4},{4,5},{5,6},{6,7},{8,9},{9,10},{10,11},{11... | collective-permute-start | bytes 73736 | tf_op jit(solution)/shard_map/ppermute | solution.py:27
  95.7 6.0 %collective-permute-start.1 = (f32[3,2048]{1,0:T(4,128)}, f32[3,2048]{1,0:T(4,128)S(1)}, u32[]{:S(2)}, u32[]{:S(2)}) collective-permute-start(f32[3,2048]{1,0:T(4,128)} %get-tuple-element.20), channel_id=1, source_target_pairs={{1,0},{2,1},{3,2},{4,3},{5,4},{6,5},{7,6},{9,8},{10,9},{11,10},{12... | collective-permute-start | bytes 73736 | tf_op jit(solution)/shard_map/ppermute | solution.py:27
  97.6 4.1 %copy-start.2 = (f32[3,2048]{1,0:T(4,128)}, f32[3,2048]{1,0:T(4,128)S(1)}, u32[]{:S(2)}) copy-start(f32[3,2048]{1,0:T(4,128)S(1)} %collective-permute-done.lower_ref) | copy-start | bytes 73732
  101.7 0.6 copy-start.3

commit v4 on v3

--- a/solution.py
+++ b/solution.py
@@ -201,12 +201,10 @@
     live_ref,
     seg_ref,
     back_ref,
-    near_rows,
     near_turn,
     near_cols,
     far_rows,
     far_turn,
-    far_cols,
     near_sum,
     far_sum,
     tile_ref,
@@ -218,25 +216,21 @@
 
     row_id = lax.broadcasted_iota(jnp.int32, (8, width), 0)
     pad = jnp.zeros((16, width), BF16)
-    gap = jnp.zeros((64, width), BF16)
 
     def operands(tile):
         one, two, three = split3(tile)
         mixed = jnp.where(row_id < 3, two, pltpu.roll(three, 3, 0))
         mixed = jnp.where(row_id < 6, mixed, 0.0)
-        columns = jnp.concatenate([one, mixed], 0)
-        return one, two, three, jnp.concatenate([columns, columns], 1).astype(BF16)
+        return one, two, three, jnp.concatenate([one, mixed], 0).astype(BF16)
 
     def prepare_near(step, carry):
         for member in range(8):
             block = 8 * step + member
             one, two, three, columns = operands(own_ref[block])
             rows = jnp.concatenate([one, one, two, two, one, three], 0).astype(BF16)
-            rows = jnp.concatenate([rows, pad], 0)
-            near_rows[block] = rows
-            near_turn[block] = jnp.concatenate([rows, gap], 0).T
-            near_cols[block] = columns
-            near_sum[block] = jnp.zeros((16, width), F32)
+            near_turn[block] = jnp.concatenate([rows, pad], 0).T
+            near_cols[block] = jnp.concatenate([columns, columns], 1)
+            near_sum[block] = jnp.zeros((width, 16), F32)
         return carry
 
     lax.fori_loop(0, blocks // 8, prepare_near, 0)
@@ -254,10 +248,8 @@
             )
             place = peer * cap + slot
             rows = jnp.concatenate([one, two, one, two, three, one], 0).astype(BF16)
-            rows = jnp.concatenate([rows, pad], 0)
-            far_rows[place] = rows
-            far_turn[place] = jnp.concatenate([gap, rows], 0).T
-            far_cols[place] = columns
+            far_rows[place] = jnp.concatenate([rows, pad], 0)
+            far_turn[place] = columns.T
             far_sum[place] = jnp.zeros((16, width), F32)
         return carry
 
@@ -269,25 +261,22 @@
             place = step * group + member
             near, far = first_ref[place], second_ref[place]
             live = live_ref[place].astype(F32)
-            right = jnp.concatenate(
-                [
-                    jnp.concatenate([far_rows[far], gap], 1),
-                    jnp.concatenate([gap, near_rows[near]], 1),
-                ],
-                0,
-            )
-            both = jnp.dot(
-                near_turn[near] + far_turn[far], right, preferred_element_type=F32
-            )
-            weight = jnp.exp2(both)
+            power = jnp.dot(near_turn[near], far_rows[far], preferred_element_type=F32)
+            weight = jnp.exp2(power)
             first = weight.astype(BF16)
             second = (weight - first.astype(F32)).astype(BF16)
-            sums = jnp.dot(
-                jnp.concatenate([near_cols[near], far_cols[far]], 0),
+            columns = far_turn[far]
+            pushed = jnp.dot(
+                jnp.concatenate([first, second], 1),
+                jnp.concatenate([columns, columns], 0),
+                preferred_element_type=F32,
+            )
+            recoil = jnp.dot(
+                near_cols[near],
                 jnp.concatenate([first, second], 0),
                 preferred_element_type=F32,
             )
-            results.append((near, far, live * sums[16:, width:], live * sums[:16, :width]))
+            results.append((near, far, live * pushed, live * recoil))
         for near, far, pushed, recoil in results:
             near_sum[near] += pushed
             far_sum[far] += recoil
@@ -302,7 +291,7 @@
     def finish_near(step, carry):
         for member in range(8):
             block = 8 * step + member
-            sums = joined(near_sum[block])
+            sums = joined(near_sum[block].T)
             seg_ref[block] = own_ref[block] * sums[4:5] - (1.0 / scale) * sums
         return carry
 
@@ -474,13 +463,11 @@
         in_specs=[VMEM, VMEM, VMEM, SMEM, SMEM, SMEM],
         out_specs=(VMEM, VMEM),
         scratch_shapes=[
-            pltpu.VMEM((blocks, 64, width), BF16),
-            pltpu.VMEM((blocks, width, width), BF16),
+            pltpu.VMEM((blocks, width, 64), BF16),
             pltpu.VMEM((blocks, 16, 2 * width), BF16),
             pltpu.VMEM((peers * cap, 64, width), BF16),
-            pltpu.VMEM((peers * cap, width, width), BF16),
-            pltpu.VMEM((peers * cap, 16, 2 * width), BF16),
-            pltpu.VMEM((blocks, 16, width), F32),
+            pltpu.VMEM((peers * cap, width, 16), BF16),
+            pltpu.VMEM((blocks, width, 16), F32),
             pltpu.VMEM((peers * cap, 16, width), F32),
             pltpu.VMEM((cap, 8, width), F32),
         ],

time: 106 us -> 162 us (1.53)
  Pallas kernels: 78.3 us -> 134 us
    pallas_call x1, Pallas kernels: 42.5 us -> 98.6 us  [shards(): pl.pallas_call(functools.partial(pair_kernel, cap, group), out_shape=(sha...]
  transfers between devices with their start and end apart: 4 -> 4, of which waited for: 3 -> 3; matrix products, arithmetic and copies ran while one was open for 0% -> 0% of each run, Pallas kernels for 21% -> 14%
where the time goes in v4:
time: 162 us; the launch traced here: 161 us
  Pallas kernels  134 us (83%)
  starting transfers between devices  17.4 us (11%)
  waiting for transfers between devices  5.44 us (3%)
  local copies, waits for them, and re-layouts  3.36 us (2%)
    pallas_call x1, Pallas kernels, shards(): pl.pallas_call(functools.partial(pair_kernel, cap, group), out_shape=(sha...  98.6 us
    pallas_call x1, Pallas kernels, shards(): pl.pallas_call(functools.partial(pull_kernel, chunk), out_shape=(shape(12...  11.9 us
    pallas_call x1, Pallas kernels, shards(): pl.pallas_call(functools.partial(force_kernel, chunk), out_shape=shape(3...  9.92 us
    all_to_all x1, starting transfers between devices, shards(): lax.all_to_all(outgoing, axes, split_axis=0, concat_axis=0, tiled=True)  7.3 us
    pallas_call x1, Pallas kernels, shards(): pl.pallas_call(functools.partial(total_kernel, cap, piece), out_shape=(sh...  6.19 us
    all_to_all x1, starting transfers between devices, shards(): lax.all_to_all(going_back, axes, split_axis=0, concat_axis=0, tiled=True)  5.84 us
    pallas_call x1, Pallas kernels, shards(): pl.pallas_call(functools.partial(segment_kernel, cap), out_shape=(shape(b...  5.02 us
    ppermute x2, waiting for transfers between devices, shifted(): lax.ppermute(value, axis, [(source, source + steps) for source in range(f...  4.72 us
  transfers between devices with their start and end apart: 4, of which 3 were waited for; matrix products, arithmetic and copies ran while one was open for 0% of the time, Pallas kernels for 14%

profile of v4, /device:TPU:0, one launch (start us, length us, event | category | flops | bytes accessed | tf_op | source)
XLA Modules:
  0.0 161.3 jit_solution(243624568510174299)
XLA Ops:
  0.6 1.4 copy.17.send_ref
  2.0 5.0 %segments.1 = (f32[64,8,128]{2,1,0:T(8,128)}, f32[32,16,128]{2,1,0:T(8,128)}) custom-call(f32[3,8192]{1,0:T(4,128)} %pos_ref.1, f32[3,8192]{1,0:T(4,128)} %disp_ref.5, s32[64,128]{1,0:T(8,128)} %seg_ref.3, s32[64,128]{1,0:T(8,128)} %mask_ref.1, s32[1,32,5]{2,1,0:T(8,128)} %copy.17.send_ref), custom_call_target="tpu_custom_call" | custom-call | tf_op jit(solution)/shard_map/segments/pallas_call | solution.py:435
  7.0 7.3 %all-to-all-start = ((f32[32,16,128]{2,1,0:T(8,128)}), f32[32,16,128]{2,1,0:T(8,128)S(1)}, u32[]{:S(2)}, u32[]{:S(2)}) async-start(f32[32,16,128]{2,1,0:T(8,128)} %get-tuple-element.13), calls=%async_computation | async-start | bytes 524288 | tf_op jit(solution)/shard_map/all_to_all | solution.py:444
  14.3 11.9 %pulls.1 = (f32[12,8192]{1,0:T(8,128)}, f32[8,128]{1,0:T(8,128)}) custom-call(f32[3,8192]{1,0:T(4,128)} %disp_ref.5, f32[1,8192]{1,0:T(1,128)} %bitcast.3, s32[4,8192]{1,0:T(4,128)} %nodes_ref.3, s32[1,8192]{1,0:T(1,128)} %bitcast.5, f32[1,8192]{1,0:T(1,128)} %bitcast.6, f32[4]{0:T(128)} %stiff_ref.1), custom_call_target="tpu_custom_call" | custom-call | flops 6442450944 | bytes 1048576 | tf_op jit(solution)/shard_map/pulls/pallas_call | solution.py:448
  26.2 0.0 all-to-all-done.got_ref
  26.2 0.0 copy-start.1
  26.2 0.7 copy-done.1
  26.9 98.6 %pairs.1 = (f32[64,8,128]{2,1,0:T(8,128)}, f32[32,16,128]{2,1,0:T(8,128)}) custom-call(f32[64,8,128]{2,1,0:T(8,128)} %get-tuple-element.12.own_ref, f32[32,16,128]{2,1,0:T(8,128)} %copy-done.1, f32[8,128]{1,0:T(8,128)} %get-tuple-element.14.ratio_ref, s32[512]{0:T(512)} %first_ref.1, s32[512]{0:T(512)} %second_ref.1, s32[512]{0:T(512)} %live_ref.1), custom_call_target="tpu_custom_call" | custom-call | tf_op jit(solution)/shard_map/pairs/pallas_call | solution.py:460
  125.5 5.8 %all-to-all-start.1 = ((f32[32,16,128]{2,1,0:T(8,128)}), f32[32,16,128]{2,1,0:T(8,128)S(1)}, u32[]{:S(2)}, u32[]{:S(2)}) async-start(f32[32,16,128]{2,1,0:T(8,128)} %get-tuple-element.15), calls=%async_computation.1 | async-start | bytes 524288 | tf_op jit(solution)/shard_map/all_to_all | solution.py:477
  131.3 9.9 %forces.1.force_ref = f32[96,256]{1,0:T(8,128)} custom-call(f32[12,8192]{1,0:T(8,128)} %get-tuple-element.17.pull_ref, s32[4,8192]{1,0:T(4,128)} %nodes_ref.3, f32[64,8,128]{2,1,0:T(8,128)} %get-tuple-element.16.after_ref.own_ref), custom_call_target="tpu_custom_call" | custom-call | flops 6442450944 | bytes 1048576 | tf_op jit(solution)/shard_map/forces/pallas_call | solution.py:479
  141.2 0.7 all-to-all-done.1.back_ref
  142.0 0.0 copy-start
  142.0 0.7 copy-done
  142.6 6.2 %totals.1 = (f32[96,256]{1,0:T(8,128)}, f32[3,2048]{1,0:T(4,128)}, f32[3,2048]{1,0:T(4,128)}, f32[8,128]{1,0:T(8,128)}) custom-call(f32[32,16,128]{2,1,0:T(8,128)} %copy-done, s32[1,32,5]{2,1,0:T(8,128)} %copy.17.send_ref, f32[64,8,128]{2,1,0:T(8,128)} %get-tuple-element.16.after_ref.own_ref, s32[64,128]{1,0:T(8,128)} %seg_ref.3, ...), custom_call_target="tpu_custom_call" | custom-call | tf_op jit(solution)/shard_map/totals/pallas_call | solution.py:490
  148.8 2.9 %collective-permute-start = (f32[3,2048]{1,0:T(4,128)}, f32[3,2048]{1,0:T(4,128)S(1)}, u32[]{:S(2)}, u32[]{:S(2)}) collective-permute-start(f32[3,2048]{1,0:T(4,128)} %get-tuple-element.19), channel_id=1, source_target_pairs={{0,1},{1,2},{2,3},{3,4},{4,5},{5,6},{6,7},{8,9},{9,10},{10,11},{11... | collective-permute-start | bytes 73736 | tf_op jit(solution)/shard_map/ppermute | solution.py:27
  151.8 1.3 collective-permute-start.1
  153.1 0.6 collective-permute-done.lower_ref
  153.7 0.0 copy-start.2
  153.7 4.1 %collective-permute-done.1.upper_ref = f32[3,2048]{1,0:T(4,128)S(1)} collective-permute-done((f32[3,2048]{1,0:T(4,128)}, f32[3,2048]{1,0:T(4,128)S(1)}, u32[]{:S(2)}, u32[]{:S(2)}) %collective-permute-start.1) | collective-permute-done | bytes 24608 | tf_op jit(solution)/shard_map/ppermute | solution.py:27
  157.8 0.0 copy-start.3
  157.8 0.0 copy-done.2
  157.8 0.6 copy-done.3
  158.4 2.9 %update.1 = (f32[3,8192]{1,0:T(4,128)}, f32[3,8192]{1,0:T(4,128)}) custom-call(f32[96,256]{1,0:T(8,128)} %get-tuple-element.18.total_ref, f32[3,2048]{1,0:T(4,128)} %copy-done.2, f32[3,2048]{1,0:T(4,128)} %copy-done.3, s32[2,2048]{1,0:T(2,128)} %shared_ref.3, f32[1,8192]{1,0:T(1,128)} %bitcast.4, f32[3,8192]{1,0:T(4,128)} %vel_ref.1, f32[3,8192]{1,0:T(4,128)} %disp_ref.5, ...), custom_call_target="tpu_custom_call" | custom-call | tf_op jit(solution)/shard_map/update/pallas_call | solution.py:502
Async XLA Ops:
  7.0 19.2 %all-to-all-start = ((f32[32,16,128]{2,1,0:T(8,128)}), f32[32,16,128]{2,1,0:T(8,128)S(1)}, u32[]{:S(2)}, u32[]{:S(2)}) async-start(f32[32,16,128]{2,1,0:T(8,128)} %get-tuple-element.13), calls=%async_computation | async-start | bytes 524288 | tf_op jit(solution)/shard_map/all_to_all | solution.py:444
  26.2 0.7 copy-start.1
  125.5 16.5 %all-to-all-start.1 = ((f32[32,16,128]{2,1,0:T(8,128)}), f32[32,16,128]{2,1,0:T(8,128)S(1)}, u32[]{:S(2)}, u32[]{:S(2)}) async-start(f32[32,16,128]{2,1,0:T(8,128)} %get-tuple-element.15), calls=%async_computation.1 | async-start | bytes 524288 | tf_op jit(solution)/shard_map/all_to_all | solution.py:477
  142.0 0.7 copy-start
  148.8 4.8 %collective-permute-start = (f32[3,2048]{1,0:T(4,128)}, f32[3,2048]{1,0:T(4,128)S(1)}, u32[]{:S(2)}, u32[]{:S(2)}) collective-permute-start(f32[3,2048]{1,0:T(4,128)} %get-tuple-element.19), channel_id=1, source_target_pairs={{0,1},{1,2},{2,3},{3,4},{4,5},{5,6},{6,7},{8,9},{9,10},{10,11},{11... | collective-permute-start | bytes 73736 | tf_op jit(solution)/shard_map/ppermute | solution.py:27
  151.8 6.0 %collective-permute-start.1 = (f32[3,2048]{1,0:T(4,128)}, f32[3,2048]{1,0:T(4,128)S(1)}, u32[]{:S(2)}, u32[]{:S(2)}) collective-permute-start(f32[3,2048]{1,0:T(4,128)} %get-tuple-element.20), channel_id=1, source_target_pairs={{1,0},{2,1},{3,2},{4,3},{5,4},{6,5},{7,6},{9,8},{10,9},{11,10},{12... | collective-permute-start | bytes 73736 | tf_op jit(solution)/shard_map/ppermute | solution.py:27
  153.7 4.1 %copy-start.2 = (f32[3,2048]{1,0:T(4,128)}, f32[3,2048]{1,0:T(4,128)S(1)}, u32[]{:S(2)}) copy-start(f32[3,2048]{1,0:T(4,128)S(1)} %collective-permute-done.lower_ref) | copy-start | bytes 73732
  157.8 0.6 copy-start.3

commit v5 on v3

--- a/solution.py
+++ b/solution.py
@@ -10,7 +10,6 @@
 
 SPRINGS = ((0, 1, 1.0), (1, 2, 1.0), (2, 3, 1.0), (3, 0, 1.0), (0, 2, 0.5), (1, 3, 0.5))
 COURANT = 0.5
-LOG2E = 1.4426950408889634
 FAR_AWAY = 64.0
 WIDE = 256
 LIMIT = 56 * 1024 * 1024
@@ -109,7 +108,7 @@
         live = lane_row(mask_ref, start, 8) > 0
         rows = [jnp.where(live, row, -FAR_AWAY) for row in pick(table, hot, mask)]
         square = rows[0] * rows[0] + rows[1] * rows[1] + rows[2] * rows[2]
-        rows += [jnp.ones_like(square), -LOG2E * square]
+        rows += [jnp.ones_like(square), -square]
         for block in range(8):
             lanes = slice(block * width, (block + 1) * width)
             for row in range(5):
@@ -214,7 +213,7 @@
     blocks, _, width = own_ref.shape
     peers = got_ref.shape[0]
     pairs = first_ref.shape[0]
-    scale = 2.0 * LOG2E
+    scale = 2.0
 
     row_id = lax.broadcasted_iota(jnp.int32, (8, width), 0)
     pad = jnp.zeros((16, width), BF16)
@@ -243,12 +242,15 @@
 
     tile_ref[...] = jnp.zeros_like(tile_ref)
 
-    def prepare_far(peer, carry):
-        for slot in range(cap):
-            tile_ref[slot, 0:3, :] = got_ref[peer, 3 * slot : 3 * slot + 3, :]
-        for slot in range(cap):
-            tile = tile_ref[slot]
-            square = -LOG2E * jnp.sum(tile * tile, 0, keepdims=True)
+    several = math.gcd(peers, 4)
+
+    def prepare_far(step, carry):
+        places = [(several * step + k, slot) for k in range(several) for slot in range(cap)]
+        for member, (peer, slot) in enumerate(places):
+            tile_ref[member, 0:3, :] = got_ref[peer, 3 * slot : 3 * slot + 3, :]
+        for member, (peer, slot) in enumerate(places):
+            tile = tile_ref[member]
+            square = -jnp.sum(tile * tile, 0, keepdims=True)
             one, two, three, columns = operands(
                 jnp.where(row_id == 3, square, jnp.where(row_id == 4, 1.0, scale * tile))
             )
@@ -261,7 +263,7 @@
             far_sum[place] = jnp.zeros((16, width), F32)
         return carry
 
-    lax.fori_loop(0, peers, prepare_far, 0)
+    lax.fori_loop(0, peers // several, prepare_far, 0)
 
     def one_group(step, carry):
         results = []
@@ -279,7 +281,7 @@
             both = jnp.dot(
                 near_turn[near] + far_turn[far], right, preferred_element_type=F32
             )
-            weight = jnp.exp2(both)
+            weight = jnp.exp(both)
             first = weight.astype(BF16)
             second = (weight - first.astype(F32)).astype(BF16)
             sums = jnp.dot(
@@ -308,17 +310,18 @@
 
     lax.fori_loop(0, blocks // 8, finish_near, 0)
 
-    def finish_far(peer, carry):
-        for slot in range(cap):
-            rows = slice(3 * slot, 3 * slot + 3)
-            sums = joined(far_sum[peer * cap + slot])
-            back_ref[peer, rows, :] = got_ref[peer, rows, :] * sums[3:4] - sums[0:3]
-        back_ref[peer, 3 * cap :, :] = jnp.broadcast_to(
-            ratio_ref[0:1], (back_ref.shape[1] - 3 * cap, width)
-        )
-        return carry
-
-    lax.fori_loop(0, peers, finish_far, 0)
+    def finish_far(step, carry):
+        for peer in [several * step + k for k in range(several)]:
+            for slot in range(cap):
+                rows = slice(3 * slot, 3 * slot + 3)
+                sums = joined(far_sum[peer * cap + slot])
+                back_ref[peer, rows, :] = got_ref[peer, rows, :] * sums[3:4] - sums[0:3]
+            back_ref[peer, 3 * cap :, :] = jnp.broadcast_to(
+                ratio_ref[0:1], (back_ref.shape[1] - 3 * cap, width)
+            )
+        return carry
+
+    lax.fori_loop(0, peers // several, finish_far, 0)
 
 
 def total_kernel(
@@ -454,7 +457,7 @@
     )(ref_pos, displacement, seg_node, seg_mask, send_blk)
     arrived = lax.all_to_all(outgoing, axes, split_axis=0, concat_axis=0, tiled=True)
 
-    chunk = math.gcd(elems, 512)
+    chunk = math.gcd(elems, 1024)
     work = 2 * 4 * elems * WIDE * depth
     pull, ratio = pl.pallas_call(
         functools.partial(pull_kernel, chunk),
@@ -467,7 +470,7 @@
         name="pulls",
     )(displacement, mass, elem_nodes, elem_part.reshape(1, -1), elem_scale.reshape(1, -1), part_stiff)
 
-    group = math.gcd(pairs, 8)
+    group = math.gcd(pairs, 32)
     seg_force, going_back = pl.pallas_call(
         functools.partial(pair_kernel, cap, group),
         out_shape=(shape(blocks, 8, width), shape(peers, slab, width)),
@@ -482,7 +485,7 @@
             pltpu.VMEM((peers * cap, 16, 2 * width), BF16),
             pltpu.VMEM((blocks, 16, width), F32),
             pltpu.VMEM((peers * cap, 16, width), F32),
-            pltpu.VMEM((cap, 8, width), F32),
+            pltpu.VMEM((4 * cap, 8, width), F32),
         ],
         compiler_params=PARAMS,
         name="pairs",

time: 106 us -> 90.1 us (0.85)
  Pallas kernels: 78.3 us -> 61.5 us
  waiting for transfers between devices: 5.5 us -> 6.79 us
    pallas_call x1, Pallas kernels: 42.5 us -> 27.4 us  [shards(): pl.pallas_call(functools.partial(pair_kernel, cap, group), out_shape=(sha...]
    all_to_all x1, waiting for transfers between devices: 0.78 us -> 2.07 us  [shards(): lax.all_to_all(going_back, axes, split_axis=0, concat_axis=0, tiled=True)]
    pallas_call x1, Pallas kernels: 9.86 us -> 8.58 us  [shards(): pl.pallas_call(functools.partial(force_kernel, chunk), out_shape=shape(3...]
  transfers between devices with their start and end apart: 4 -> 4, of which waited for: 3 -> 3; matrix products, arithmetic and copies ran while one was open for 0% -> 0% of each run, Pallas kernels for 21% -> 22%
where the time goes in v5:
time: 90.1 us; the launch traced here: 89.6 us
  Pallas kernels  61.5 us (68%)
  starting transfers between devices  17.3 us (19%)
  waiting for transfers between devices  6.79 us (8%)
  local copies, waits for them, and re-layouts  3.36 us (4%)
    pallas_call x1, Pallas kernels, shards(): pl.pallas_call(functools.partial(pair_kernel, cap, group), out_shape=(sha...  27.4 us
    pallas_call x1, Pallas kernels, shards(): pl.pallas_call(functools.partial(pull_kernel, chunk), out_shape=(shape(12...  11.4 us
    pallas_call x1, Pallas kernels, shards(): pl.pallas_call(functools.partial(force_kernel, chunk), out_shape=shape(3...  8.58 us
    all_to_all x1, starting transfers between devices, shards(): lax.all_to_all(outgoing, axes, split_axis=0, concat_axis=0, tiled=True)  7.3 us
    pallas_call x1, Pallas kernels, shards(): pl.pallas_call(functools.partial(total_kernel, cap, piece), out_shape=(sh...  6.19 us
    all_to_all x1, starting transfers between devices, shards(): lax.all_to_all(going_back, axes, split_axis=0, concat_axis=0, tiled=True)  5.83 us
    pallas_call x1, Pallas kernels, shards(): pl.pallas_call(functools.partial(segment_kernel, cap), out_shape=(shape(b...  5.02 us
    ppermute x2, waiting for transfers between devices, shifted(): lax.ppermute(value, axis, [(source, source + steps) for source in range(f...  4.72 us
  transfers between devices with their start and end apart: 4, of which 3 were waited for; matrix products, arithmetic and copies ran while one was open for 0% of the time, Pallas kernels for 22%

profile of v5, /device:TPU:0, one launch (start us, length us, event | category | flops | bytes accessed | tf_op | source)
XLA Modules:
  0.0 89.6 jit_solution(5949870088074092549)
XLA Ops:
  0.6 1.4 %copy.17.send_ref = s32[1,32,5]{2,1,0:T(8,128)} copy(s32[1,32,5]{1,0,2:T(1,128)} %param.26) | data formatting | bytes 1280 | tf_op args[11]
  2.0 5.0 %segments.1 = (f32[64,8,128]{2,1,0:T(8,128)}, f32[32,16,128]{2,1,0:T(8,128)}) custom-call(f32[3,8192]{1,0:T(4,128)} %pos_ref.1, f32[3,8192]{1,0:T(4,128)} %disp_ref.5, s32[64,128]{1,0:T(8,128)} %seg_ref.3, s32[64,128]{1,0:T(8,128)} %mask_ref.1, s32[1,32,5]{2,1,0:T(8,128)} %copy.17.send_ref), custom_call_target="tpu_custom_call" | custom-call | tf_op jit(solution)/shard_map/segments/pallas_call | solution.py:449
  7.0 7.3 %all-to-all-start = ((f32[32,16,128]{2,1,0:T(8,128)}), f32[32,16,128]{2,1,0:T(8,128)S(1)}, u32[]{:S(2)}, u32[]{:S(2)}) async-start(f32[32,16,128]{2,1,0:T(8,128)} %get-tuple-element.13), calls=%async_computation | async-start | bytes 524288 | tf_op jit(solution)/shard_map/all_to_all | solution.py:458
  14.3 11.4 %pulls.1 = (f32[12,8192]{1,0:T(8,128)}, f32[8,128]{1,0:T(8,128)}) custom-call(f32[3,8192]{1,0:T(4,128)} %disp_ref.5, f32[1,8192]{1,0:T(1,128)} %bitcast.3, s32[4,8192]{1,0:T(4,128)} %nodes_ref.3, s32[1,8192]{1,0:T(1,128)} %bitcast.5, f32[1,8192]{1,0:T(1,128)} %bitcast.6, f32[4]{0:T(128)} %stiff_ref.1), custom_call_target="tpu_custom_call" | custom-call | flops 6442450944 | bytes 1048576 | tf_op jit(solution)/shard_map/pulls/pallas_call | solution.py:462
  25.7 0.0 all-to-all-done.got_ref
  25.7 0.0 copy-start.1
  25.8 0.7 copy-done.1
  26.4 27.4 %pairs.1 = (f32[64,8,128]{2,1,0:T(8,128)}, f32[32,16,128]{2,1,0:T(8,128)}) custom-call(f32[64,8,128]{2,1,0:T(8,128)} %get-tuple-element.12.own_ref, f32[32,16,128]{2,1,0:T(8,128)} %copy-done.1, f32[8,128]{1,0:T(8,128)} %get-tuple-element.14.ratio_ref, s32[512]{0:T(512)} %first_ref.1, s32[512]{0:T(512)} %second_ref.1, s32[512]{0:T(512)} %live_ref.1), custom_call_target="tpu_custom_call" | custom-call | tf_op jit(solution)/shard_map/pairs/pallas_call | solution.py:474
  53.8 5.8 %all-to-all-start.1 = ((f32[32,16,128]{2,1,0:T(8,128)}), f32[32,16,128]{2,1,0:T(8,128)S(1)}, u32[]{:S(2)}, u32[]{:S(2)}) async-start(f32[32,16,128]{2,1,0:T(8,128)} %get-tuple-element.15), calls=%async_computation.1 | async-start | bytes 524288 | tf_op jit(solution)/shard_map/all_to_all | solution.py:493
  59.7 8.6 %forces.1.force_ref = f32[96,256]{1,0:T(8,128)} custom-call(f32[12,8192]{1,0:T(8,128)} %get-tuple-element.17.pull_ref, s32[4,8192]{1,0:T(4,128)} %nodes_ref.3, f32[64,8,128]{2,1,0:T(8,128)} %get-tuple-element.16.after_ref.own_ref), custom_call_target="tpu_custom_call" | custom-call | flops 6442450944 | bytes 1048576 | tf_op jit(solution)/shard_map/forces/pallas_call | solution.py:495
  68.2 2.1 %all-to-all-done.1.back_ref = f32[32,16,128]{2,1,0:T(8,128)S(1)} async-done(((f32[32,16,128]{2,1,0:T(8,128)}), f32[32,16,128]{2,1,0:T(8,128)S(1)}, u32[]{:S(2)}, u32[]{:S(2)}) %all-to-all-start.1) | async-done | bytes 262176 | tf_op jit(solution)/shard_map/all_to_all | solution.py:493
  70.3 0.0 copy-start
  70.3 0.7 copy-done
  71.0 6.2 %totals.1 = (f32[96,256]{1,0:T(8,128)}, f32[3,2048]{1,0:T(4,128)}, f32[3,2048]{1,0:T(4,128)}, f32[8,128]{1,0:T(8,128)}) custom-call(f32[32,16,128]{2,1,0:T(8,128)} %copy-done, s32[1,32,5]{2,1,0:T(8,128)} %copy.17.send_ref, f32[64,8,128]{2,1,0:T(8,128)} %get-tuple-element.16.after_ref.own_ref, s32[64,128]{1,0:T(8,128)} %seg_ref.3, ...), custom_call_target="tpu_custom_call" | custom-call | tf_op jit(solution)/shard_map/totals/pallas_call | solution.py:506
  77.2 2.9 %collective-permute-start = (f32[3,2048]{1,0:T(4,128)}, f32[3,2048]{1,0:T(4,128)S(1)}, u32[]{:S(2)}, u32[]{:S(2)}) collective-permute-start(f32[3,2048]{1,0:T(4,128)} %get-tuple-element.19), channel_id=1, source_target_pairs={{0,1},{1,2},{2,3},{3,4},{4,5},{5,6},{6,7},{8,9},{9,10},{10,11},{11... | collective-permute-start | bytes 73736 | tf_op jit(solution)/shard_map/ppermute | solution.py:26
  80.1 1.3 %collective-permute-start.1 = (f32[3,2048]{1,0:T(4,128)}, f32[3,2048]{1,0:T(4,128)S(1)}, u32[]{:S(2)}, u32[]{:S(2)}) collective-permute-start(f32[3,2048]{1,0:T(4,128)} %get-tuple-element.20), channel_id=1, source_target_pairs={{1,0},{2,1},{3,2},{4,3},{5,4},{6,5},{7,6},{9,8},{10,9},{11,10},{12... | collective-permute-start | bytes 73736 | tf_op jit(solution)/shard_map/ppermute | solution.py:26
  81.4 0.6 collective-permute-done.lower_ref
  82.0 0.0 copy-start.2
  82.0 4.1 %collective-permute-done.1.upper_ref = f32[3,2048]{1,0:T(4,128)S(1)} collective-permute-done((f32[3,2048]{1,0:T(4,128)}, f32[3,2048]{1,0:T(4,128)S(1)}, u32[]{:S(2)}, u32[]{:S(2)}) %collective-permute-start.1) | collective-permute-done | bytes 24608 | tf_op jit(solution)/shard_map/ppermute | solution.py:26
  86.1 0.0 copy-start.3
  86.1 0.0 copy-done.2
  86.1 0.6 copy-done.3
  86.7 2.9 %update.1 = (f32[3,8192]{1,0:T(4,128)}, f32[3,8192]{1,0:T(4,128)}) custom-call(f32[96,256]{1,0:T(8,128)} %get-tuple-element.18.total_ref, f32[3,2048]{1,0:T(4,128)} %copy-done.2, f32[3,2048]{1,0:T(4,128)} %copy-done.3, s32[2,2048]{1,0:T(2,128)} %shared_ref.3, f32[1,8192]{1,0:T(1,128)} %bitcast.4, f32[3,8192]{1,0:T(4,128)} %vel_ref.1, f32[3,8192]{1,0:T(4,128)} %disp_ref.5, ...), custom_call_target="tpu_custom_call" | custom-call | tf_op jit(solution)/shard_map/update/pallas_call | solution.py:518
Async XLA Ops:
  7.0 18.7 %all-to-all-start = ((f32[32,16,128]{2,1,0:T(8,128)}), f32[32,16,128]{2,1,0:T(8,128)S(1)}, u32[]{:S(2)}, u32[]{:S(2)}) async-start(f32[32,16,128]{2,1,0:T(8,128)} %get-tuple-element.13), calls=%async_computation | async-start | bytes 524288 | tf_op jit(solution)/shard_map/all_to_all | solution.py:458
  25.7 0.7 copy-start.1
  53.8 16.5 %all-to-all-start.1 = ((f32[32,16,128]{2,1,0:T(8,128)}), f32[32,16,128]{2,1,0:T(8,128)S(1)}, u32[]{:S(2)}, u32[]{:S(2)}) async-start(f32[32,16,128]{2,1,0:T(8,128)} %get-tuple-element.15), calls=%async_computation.1 | async-start | bytes 524288 | tf_op jit(solution)/shard_map/all_to_all | solution.py:493
  70.3 0.7 copy-start
  77.2 4.8 %collective-permute-start = (f32[3,2048]{1,0:T(4,128)}, f32[3,2048]{1,0:T(4,128)S(1)}, u32[]{:S(2)}, u32[]{:S(2)}) collective-permute-start(f32[3,2048]{1,0:T(4,128)} %get-tuple-element.19), channel_id=1, source_target_pairs={{0,1},{1,2},{2,3},{3,4},{4,5},{5,6},{6,7},{8,9},{9,10},{10,11},{11... | collective-permute-start | bytes 73736 | tf_op jit(solution)/shard_map/ppermute | solution.py:26
  80.1 6.0 %collective-permute-start.1 = (f32[3,2048]{1,0:T(4,128)}, f32[3,2048]{1,0:T(4,128)S(1)}, u32[]{:S(2)}, u32[]{:S(2)}) collective-permute-start(f32[3,2048]{1,0:T(4,128)} %get-tuple-element.20), channel_id=1, source_target_pairs={{1,0},{2,1},{3,2},{4,3},{5,4},{6,5},{7,6},{9,8},{10,9},{11,10},{12... | collective-permute-start | bytes 73736 | tf_op jit(solution)/shard_map/ppermute | solution.py:26
  82.0 4.1 %copy-start.2 = (f32[3,2048]{1,0:T(4,128)}, f32[3,2048]{1,0:T(4,128)S(1)}, u32[]{:S(2)}) copy-start(f32[3,2048]{1,0:T(4,128)S(1)} %collective-permute-done.lower_ref) | copy-start | bytes 73732
  86.1 0.6 copy-start.3

commit v6 on v5

--- a/solution.py
+++ b/solution.py
@@ -20,12 +20,6 @@
 PARAMS = pltpu.CompilerParams(vmem_limit_bytes=LIMIT)
 
 
-def shifted(value, axis, steps):
-    count = lax.axis_size(axis)
-    first, last = (max(0, -steps), min(count, count - steps))
-    return lax.ppermute(value, axis, [(source, source + steps) for source in range(first, last)])
-
-
 def split3(x):
     first = x.astype(BF16).astype(F32)
     rest = x - first
@@ -102,32 +96,37 @@
     fold(moved_ref, table_ref)
     table = split_table(table_ref[...])
 
+    many = math.gcd(blocks, 16)
+
     def gather(step, carry):
-        start = step * 8
-        hot, mask = selectors(lane_row(seg_ref, start, 8), depth)
-        live = lane_row(mask_ref, start, 8) > 0
+        start = step * many
+        hot, mask = selectors(lane_row(seg_ref, start, many), depth)
+        live = lane_row(mask_ref, start, many) > 0
         rows = [jnp.where(live, row, -FAR_AWAY) for row in pick(table, hot, mask)]
         square = rows[0] * rows[0] + rows[1] * rows[1] + rows[2] * rows[2]
         rows += [jnp.ones_like(square), -square]
-        for block in range(8):
+        for block in range(many):
             lanes = slice(block * width, (block + 1) * width)
             for row in range(5):
                 own_ref[start + block, row : row + 1, :] = rows[row][:, lanes]
             own_ref[start + block, 5:8, :] = jnp.zeros((3, width), F32)
         return carry
 
-    lax.fori_loop(0, blocks // 8, gather, 0)
-
-    def send(peer, carry):
-        for slot in range(cap):
-            block = own_ref[send_ref[0, peer, slot], 0:3, :]
-            out_ref[peer, 3 * slot : 3 * slot + 3, :] = jnp.where(
-                block < -0.5 * FAR_AWAY, FAR_AWAY, block
-            )
-        out_ref[peer, 3 * cap :, :] = jnp.zeros((out_ref.shape[1] - 3 * cap, width), F32)
-        return carry
-
-    lax.fori_loop(0, out_ref.shape[0], send, 0)
+    lax.fori_loop(0, blocks // many, gather, 0)
+
+    several = math.gcd(out_ref.shape[0], 8)
+
+    def send(step, carry):
+        for peer in [several * step + k for k in range(several)]:
+            for slot in range(cap):
+                block = own_ref[send_ref[peer * cap + slot], 0:3, :]
+                out_ref[peer, 3 * slot : 3 * slot + 3, :] = jnp.where(
+                    block < -0.5 * FAR_AWAY, FAR_AWAY, block
+                )
+            out_ref[peer, 3 * cap :, :] = jnp.zeros((out_ref.shape[1] - 3 * cap, width), F32)
+        return carry
+
+    lax.fori_loop(0, out_ref.shape[0] // several, send, 0)
 
 
 def pull_kernel(
@@ -343,39 +342,46 @@
     blocks, width = seg_ref.shape
     sums[...] = own_ref[...]
 
-    def give_back(peer, best):
-        for slot in range(cap):
-            block = send_ref[0, peer, slot]
-            sums[block, 0:3, :] += back_ref[peer, 3 * slot : 3 * slot + 3, :]
-        return jnp.minimum(best, back_ref[peer, 3 * cap : 3 * cap + 1, :])
+    peers = back_ref.shape[0]
+    several = math.gcd(peers, 8)
+
+    def give_back(step, best):
+        for peer in [several * step + k for k in range(several)]:
+            for slot in range(cap):
+                block = send_ref[peer * cap + slot]
+                sums[block, 0:3, :] += back_ref[peer, 3 * slot : 3 * slot + 3, :]
+            best = jnp.minimum(best, back_ref[peer, 3 * cap : 3 * cap + 1, :])
+        return best
 
     best = lax.fori_loop(
-        0, back_ref.shape[0], give_back, jnp.full((1, width), jnp.inf, F32)
+        0, peers // several, give_back, jnp.full((1, width), jnp.inf, F32)
     )
     step_ref[...] = jnp.broadcast_to(COURANT * jnp.sqrt(best), step_ref.shape)
     total_ref[...] = force_ref[...]
 
+    many = math.gcd(blocks, 16)
+
     def scatter(step, carry):
-        start = step * 8
-        hot, mask = selectors(lane_row(seg_ref, start, 8), depth)
+        start = step * many
+        hot, mask = selectors(lane_row(seg_ref, start, many), depth)
         rows = [
-            jnp.concatenate([sums[start + block, row : row + 1, :] for block in range(8)], 1)
+            jnp.concatenate([sums[start + block, row : row + 1, :] for block in range(many)], 1)
             for row in range(3)
         ]
         total_ref[...] += spread(rows, hot, mask)
         return carry
 
-    lax.fori_loop(0, blocks // 8, scatter, 0)
+    lax.fori_loop(0, blocks // many, scatter, 0)
 
     table = split_table(total_ref[...])
 
     def gather(step, carry):
         lanes = pl.ds(pl.multiple_of(step * chunk, chunk), chunk)
-        for side, out_ref in ((0, upper_ref), (1, lower_ref)):
-            hot, mask = selectors(shared_ref[side : side + 1, lanes], depth)
-            rows = pick(table, hot, mask)
-            for row in range(3):
-                out_ref[row : row + 1, lanes] = rows[row]
+        index = jnp.concatenate([shared_ref[side : side + 1, lanes] for side in range(2)], 1)
+        rows = pick(table, *selectors(index, depth))
+        for row in range(3):
+            upper_ref[row : row + 1, lanes] = rows[row][:, :chunk]
+            lower_ref[row : row + 1, lanes] = rows[row][:, chunk:]
         return carry
 
     lax.fori_loop(0, shared_ref.shape[1] // chunk, gather, 0)
@@ -394,16 +400,78 @@
     new_disp_ref,
     new_vel_ref,
     sums,
+    got_lower,
+    got_upper,
+    sent,
+    received,
 ):
+    me = lax.axis_index("dev")
+    last = lax.axis_size("dev") - 1
+    prev = {"dev": jnp.maximum(me - 1, 0)}
+    following = {"dev": jnp.minimum(me + 1, last)}
+    upward = pltpu.make_async_remote_copy(
+        src_ref=lower_ref,
+        dst_ref=got_lower,
+        send_sem=sent.at[0],
+        recv_sem=received.at[0],
+        device_id=following,
+        device_id_type=pl.DeviceIdType.MESH,
+    )
+    downward = pltpu.make_async_remote_copy(
+        src_ref=upper_ref,
+        dst_ref=got_upper,
+        send_sem=sent.at[1],
+        recv_sem=received.at[1],
+        device_id=prev,
+        device_id_type=pl.DeviceIdType.MESH,
+    )
+    barrier = pltpu.get_barrier_semaphore()
+
+    @pl.when(me > 0)
+    def _():
+        pl.semaphore_signal(barrier, 1, device_id=prev, device_id_type=pl.DeviceIdType.MESH)
+
+    @pl.when(me < last)
+    def _():
+        pl.semaphore_signal(barrier, 1, device_id=following, device_id_type=pl.DeviceIdType.MESH)
+
+    pl.semaphore_wait(barrier, jnp.minimum(me, 1) + jnp.minimum(last - me, 1))
+
+    @pl.when(me < last)
+    def _():
+        upward.start()
+
+    @pl.when(me > 0)
+    def _():
+        downward.start()
+
     sums[...] = total_ref[...]
     depth = sums.shape[0] // 3
 
+    @pl.when(me == 0)
+    def _():
+        got_lower[...] = jnp.zeros_like(got_lower)
+
+    @pl.when(me == last)
+    def _():
+        got_upper[...] = jnp.zeros_like(got_upper)
+
+    @pl.when(me > 0)
+    def _():
+        upward.wait_recv()
+
+    @pl.when(me < last)
+    def _():
+        downward.wait_recv()
+
     def scatter(step, carry):
         lanes = pl.ds(pl.multiple_of(step * chunk, chunk), chunk)
-        for side, in_ref in ((0, lower_ref), (1, upper_ref)):
-            hot, mask = selectors(shared_ref[side : side + 1, lanes], depth)
-            rows = [in_ref[row : row + 1, lanes] for row in range(3)]
-            sums[...] += spread(rows, hot, mask)
+        index = jnp.concatenate([shared_ref[side : side + 1, lanes] for side in range(2)], 1)
+        rows = [
+            jnp.concatenate([got_lower[row : row + 1, lanes], got_upper[row : row + 1, lanes]], 1)
+            for row in range(3)
+        ]
+        sums[...] += spread(rows, *selectors(index, depth))
         return carry
 
     lax.fori_loop(0, shared_ref.shape[1] // chunk, scatter, 0)
@@ -412,6 +480,14 @@
     velocity = vel_ref[...] + time_step * (new_vel_ref[...] / mass_ref[...])
     new_vel_ref[...] = velocity
     new_disp_ref[...] = disp_ref[...] + time_step * velocity
+
+    @pl.when(me < last)
+    def _():
+        upward.wait_send()
+
+    @pl.when(me > 0)
+    def _():
+        downward.wait_send()
 
 
 def shape(*dims):
@@ -445,6 +521,7 @@
     depth = nodes // WIDE
     slab = -(-(3 * cap + 1) // 8) * 8
     mass = node_mass.reshape(1, -1)
+    send = send_blk.reshape(-1)
 
     own, outgoing = pl.pallas_call(
         functools.partial(segment_kernel, cap),
@@ -454,7 +531,7 @@
         scratch_shapes=[pltpu.VMEM((3 * depth, WIDE), F32), pltpu.VMEM((3, nodes), F32)],
         compiler_params=PARAMS,
         name="segments",
-    )(ref_pos, displacement, seg_node, seg_mask, send_blk)
+    )(ref_pos, displacement, seg_node, seg_mask, send)
     arrived = lax.all_to_all(outgoing, axes, split_axis=0, concat_axis=0, tiled=True)
 
     chunk = math.gcd(elems, 1024)
@@ -470,7 +547,7 @@
         name="pulls",
     )(displacement, mass, elem_nodes, elem_part.reshape(1, -1), elem_scale.reshape(1, -1), part_stiff)
 
-    group = math.gcd(pairs, 32)
+    group = math.gcd(pairs, 64)
     seg_force, going_back = pl.pallas_call(
         functools.partial(pair_kernel, cap, group),
         out_shape=(shape(blocks, 8, width), shape(peers, slab, width)),
@@ -502,7 +579,7 @@
         name="forces",
     )(pull, elem_nodes, seg_force)
 
-    piece = math.gcd(share, 1024)
+    piece = math.gcd(share, 2048)
     total, lower, upper, time_step = pl.pallas_call(
         functools.partial(total_kernel, cap, piece),
         out_shape=(shape(3 * depth, WIDE), shape(3, share), shape(3, share), shape(8, width)),
@@ -511,19 +588,25 @@
         scratch_shapes=[pltpu.VMEM((blocks, 8, width), F32)],
         compiler_params=PARAMS,
         name="totals",
-    )(returned, send_blk, seg_force, seg_node, force, shared)
-    from_lower = shifted(lower, "dev", 1)
-    from_upper = shifted(upper, "dev", -1)
+    )(returned, send, seg_force, seg_node, force, shared)
 
     return pl.pallas_call(
         functools.partial(update_kernel, piece),
         out_shape=(shape(3, nodes), shape(3, nodes)),
         in_specs=[VMEM] * 8,
         out_specs=(VMEM, VMEM),
-        scratch_shapes=[pltpu.VMEM((3 * depth, WIDE), F32)],
-        compiler_params=PARAMS,
+        scratch_shapes=[
+            pltpu.VMEM((3 * depth, WIDE), F32),
+            pltpu.VMEM((3, share), F32),
+            pltpu.VMEM((3, share), F32),
+            pltpu.SemaphoreType.DMA((2,)),
+            pltpu.SemaphoreType.DMA((2,)),
+        ],
+        compiler_params=pltpu.CompilerParams(
+            vmem_limit_bytes=LIMIT, collective_id=0, has_side_effects=True
+        ),
         name="update",
-    )(total, from_lower, from_upper, shared, mass, velocity, displacement, time_step)
+    )(total, lower, upper, shared, mass, velocity, displacement, time_step)
 
 
 def solution(mesh):

time: 90.1 us -> 83.4 us (0.926)
  waiting for transfers between devices: 6.79 us -> 2.07 us
  starting transfers between devices: 17.3 us -> 13.1 us
  local copies, waits for them, and re-layouts: 3.36 us -> 5.12 us
    ppermute x2 -> x0, waiting for transfers between devices: 4.72 us -> none  [shifted(): lax.ppermute(value, axis, [(source, source + steps) for source in range(f...]
    ppermute x2 -> x0, starting transfers between devices: 4.19 us -> none  [shifted(): lax.ppermute(value, axis, [(source, source + steps) for source in range(f...]
    pallas_call x1, Pallas kernels: 2.92 us -> 7.07 us  [shards(): pl.pallas_call(functools.partial(update_kernel, piece), out_shape=(shape(...]
    pallas_call x1, Pallas kernels: 27.4 us -> 25.2 us  [shards(): pl.pallas_call(functools.partial(pair_kernel, cap, group), out_shape=(sha...]
    unnamed x9, local copies, waits for them, and re-layouts: 3.36 us -> 4.44 us
  transfers between devices with their start and end apart: 4 -> 2, of which waited for: 3 -> 1; matrix products, arithmetic and copies ran while one was open for 0% -> 0% of each run, Pallas kernels for 22% -> 24%
where the time goes in v6:
time: 83.4 us; the launch traced here: 83 us
  Pallas kernels  62 us (74%)
  starting transfers between devices  13.1 us (16%)
  local copies, waits for them, and re-layouts  5.12 us (6%)
  waiting for transfers between devices  2.07 us (2%)
    pallas_call x1, Pallas kernels, shards(): pl.pallas_call(functools.partial(pair_kernel, cap, group), out_shape=(sha...  25.2 us
    pallas_call x1, Pallas kernels, shards(): pl.pallas_call(functools.partial(pull_kernel, chunk), out_shape=(shape(12...  11.4 us
    pallas_call x1, Pallas kernels, shards(): pl.pallas_call(functools.partial(force_kernel, chunk), out_shape=shape(3...  8.58 us
    all_to_all x1, starting transfers between devices, shards(): lax.all_to_all(outgoing, axes, split_axis=0, concat_axis=0, tiled=True)  7.3 us
    pallas_call x1, Pallas kernels, shards(): pl.pallas_call(functools.partial(update_kernel, piece), out_shape=(shape(...  7.07 us
    all_to_all x1, starting transfers between devices, shards(): lax.all_to_all(going_back, axes, split_axis=0, concat_axis=0, tiled=True)  5.83 us
    pallas_call x1, Pallas kernels, shards(): pl.pallas_call(functools.partial(total_kernel, cap, piece), out_shape=(sh...  5.52 us
    unnamed x9, local copies, waits for them, and re-layouts  4.44 us
  transfers between devices with their start and end apart: 2, of which 1 were waited for; matrix products, arithmetic and copies ran while one was open for 0% of the time, Pallas kernels for 24%

profile of v6, /device:TPU:0, one launch (start us, length us, event | category | flops | bytes accessed | tf_op | source)
XLA Modules:
  0.0 83.0 jit_solution(7799498672491345602)
XLA Ops:
  0.6 0.8 copy.17
  1.4 0.7 reshape.16.send_ref
  2.1 4.3 %segments.1 = (f32[64,8,128]{2,1,0:T(8,128)}, f32[32,16,128]{2,1,0:T(8,128)}) custom-call(f32[3,8192]{1,0:T(4,128)} %pos_ref.1, f32[3,8192]{1,0:T(4,128)} %disp_ref.5, s32[64,128]{1,0:T(8,128)} %seg_ref.3, s32[64,128]{1,0:T(8,128)} %mask_ref.1, s32[160]{0:T(256)} %reshape.16.send_ref), custom_call_target="tpu_custom_call" | custom-call | tf_op jit(solution)/shard_map/segments/pallas_call | solution.py:526
  6.4 7.3 %all-to-all-start = ((f32[32,16,128]{2,1,0:T(8,128)}), f32[32,16,128]{2,1,0:T(8,128)S(1)}, u32[]{:S(2)}, u32[]{:S(2)}) async-start(f32[32,16,128]{2,1,0:T(8,128)} %get-tuple-element.13), calls=%async_computation | async-start | bytes 524288 | tf_op jit(solution)/shard_map/all_to_all | solution.py:535
  13.7 11.4 %pulls.1 = (f32[12,8192]{1,0:T(8,128)}, f32[8,128]{1,0:T(8,128)}) custom-call(f32[3,8192]{1,0:T(4,128)} %disp_ref.5, f32[1,8192]{1,0:T(1,128)} %bitcast.3, s32[4,8192]{1,0:T(4,128)} %nodes_ref.3, s32[1,8192]{1,0:T(1,128)} %bitcast.5, f32[1,8192]{1,0:T(1,128)} %bitcast.6, f32[4]{0:T(128)} %stiff_ref.1), custom_call_target="tpu_custom_call" | custom-call | flops 6442450944 | bytes 1048576 | tf_op jit(solution)/shard_map/pulls/pallas_call | solution.py:539
  25.1 0.0 all-to-all-done.got_ref
  25.1 0.0 copy-start.1
  25.1 0.7 copy-done.1
  25.8 25.2 %pairs.1 = (f32[64,8,128]{2,1,0:T(8,128)}, f32[32,16,128]{2,1,0:T(8,128)}) custom-call(f32[64,8,128]{2,1,0:T(8,128)} %get-tuple-element.12.own_ref, f32[32,16,128]{2,1,0:T(8,128)} %copy-done.1, f32[8,128]{1,0:T(8,128)} %get-tuple-element.14.ratio_ref, s32[512]{0:T(512)} %first_ref.1, s32[512]{0:T(512)} %second_ref.1, s32[512]{0:T(512)} %live_ref.1), custom_call_target="tpu_custom_call" | custom-call | tf_op jit(solution)/shard_map/pairs/pallas_call | solution.py:551
  51.0 5.8 %all-to-all-start.1 = ((f32[32,16,128]{2,1,0:T(8,128)}), f32[32,16,128]{2,1,0:T(8,128)S(1)}, u32[]{:S(2)}, u32[]{:S(2)}) async-start(f32[32,16,128]{2,1,0:T(8,128)} %get-tuple-element.15), calls=%async_computation.1 | async-start | bytes 524288 | tf_op jit(solution)/shard_map/all_to_all | solution.py:570
  56.8 8.6 %forces.1.force_ref = f32[96,256]{1,0:T(8,128)} custom-call(f32[12,8192]{1,0:T(8,128)} %get-tuple-element.17.pull_ref, s32[4,8192]{1,0:T(4,128)} %nodes_ref.3, f32[64,8,128]{2,1,0:T(8,128)} %get-tuple-element.16.after_ref.own_ref), custom_call_target="tpu_custom_call" | custom-call | flops 6442450944 | bytes 1048576 | tf_op jit(solution)/shard_map/forces/pallas_call | solution.py:572
  65.4 2.1 %all-to-all-done.1.back_ref = f32[32,16,128]{2,1,0:T(8,128)S(1)} async-done(((f32[32,16,128]{2,1,0:T(8,128)}), f32[32,16,128]{2,1,0:T(8,128)S(1)}, u32[]{:S(2)}, u32[]{:S(2)}) %all-to-all-start.1) | async-done | bytes 262176 | tf_op jit(solution)/shard_map/all_to_all | solution.py:570
  67.5 0.0 copy-start
  67.5 0.7 copy-done
  68.2 5.5 %totals.1 = (f32[96,256]{1,0:T(8,128)}, f32[3,2048]{1,0:T(4,128)}, f32[3,2048]{1,0:T(4,128)}, f32[8,128]{1,0:T(8,128)}) custom-call(f32[32,16,128]{2,1,0:T(8,128)} %copy-done, s32[160]{0:T(256)} %reshape.16.send_ref, f32[64,8,128]{2,1,0:T(8,128)} %get-tuple-element.16.after_ref.own_ref, s32[64,128]{1,0:T(8,128)} %seg_ref.3, f32[96,256]{1,0:T(8,128)} %forces.1.force_ref, ...), custom_call_target="tpu_custom_call" | custom-call | tf_op jit(solution)/shard_map/totals/pallas_call | solution.py:583
  73.7 7.1 %update.1 = (f32[3,8192]{1,0:T(4,128)}, f32[3,8192]{1,0:T(4,128)}) custom-call(f32[96,256]{1,0:T(8,128)} %get-tuple-element.18.total_ref, f32[3,2048]{1,0:T(4,128)} %get-tuple-element.19.lower_ref, f32[3,2048]{1,0:T(4,128)} %get-tuple-element.20.upper_ref, s32[2,2048]{1,0:T(2,128)} %shared_ref.3, f32[1,8192]{1,0:T(1,128)} %bitcast.4, f32[3,8192]{1,0:T(4,128)} %vel_ref.1, ...), custom_call_target="tpu_custom_call" | custom-call | tf_op jit(solution)/shard_map/update/pallas_call | solution.py:593
  80.8 0.0 copy-start.2
  80.8 1.6 %copy.20 = f32[3,8192]{1,0:T(4,128)} copy(f32[3,8192]{1,0:T(4,128)} %get-tuple-element.24) | data formatting | bytes 196608
  82.4 0.0 copy-done.2
  82.4 0.7 copy.21
Async XLA Ops:
  6.4 18.7 %all-to-all-start = ((f32[32,16,128]{2,1,0:T(8,128)}), f32[32,16,128]{2,1,0:T(8,128)S(1)}, u32[]{:S(2)}, u32[]{:S(2)}) async-start(f32[32,16,128]{2,1,0:T(8,128)} %get-tuple-element.13), calls=%async_computation | async-start | bytes 524288 | tf_op jit(solution)/shard_map/all_to_all | solution.py:535
  25.1 0.7 copy-start.1
  51.0 16.5 %all-to-all-start.1 = ((f32[32,16,128]{2,1,0:T(8,128)}), f32[32,16,128]{2,1,0:T(8,128)S(1)}, u32[]{:S(2)}, u32[]{:S(2)}) async-start(f32[32,16,128]{2,1,0:T(8,128)} %get-tuple-element.15), calls=%async_computation.1 | async-start | bytes 524288 | tf_op jit(solution)/shard_map/all_to_all | solution.py:570
  67.5 0.7 copy-start
  80.8 1.6 %copy-start.2 = (f32[3,8192]{1,0:T(4,128)S(1)}, f32[3,8192]{1,0:T(4,128)}, u32[]{:S(2)}) copy-start(f32[3,8192]{1,0:T(4,128)} %get-tuple-element.25) | copy-start | bytes 294916

commit v7 on v6

--- a/solution.py
+++ b/solution.py
@@ -85,6 +85,56 @@
 def lane_row(ref, start, count):
     tile = ref[pl.ds(pl.multiple_of(start, 8), count), :]
     return jnp.concatenate([tile[row : row + 1] for row in range(count)], 1)
+
+
+def exchange(out_ref, got_ref, sent, received, kept):
+    within = lax.axis_size("dev")
+    count = lax.axis_size("grp") * within
+    me = lax.axis_index("grp") * within + lax.axis_index("dev")
+
+    def place(index):
+        return {"grp": lax.div(index, within), "dev": lax.rem(index, within)}
+
+    def copy(offset, landing):
+        target = lax.rem(me + offset, count)
+        return pltpu.make_async_remote_copy(
+            src_ref=out_ref.at[target],
+            dst_ref=got_ref.at[landing],
+            send_sem=sent.at[offset],
+            recv_sem=received.at[offset],
+            device_id=place(target),
+            device_id_type=pl.DeviceIdType.MESH,
+        )
+
+    barrier = pltpu.get_barrier_semaphore()
+
+    def greet(offset, carry):
+        target = lax.rem(me + offset, count)
+        pl.semaphore_signal(
+            barrier, 1, device_id=place(target), device_id_type=pl.DeviceIdType.MESH
+        )
+        return carry
+
+    lax.fori_loop(1, count, greet, 0)
+    own = pltpu.make_async_copy(out_ref.at[me], got_ref.at[me], kept)
+    own.start()
+    pl.semaphore_wait(barrier, count - 1)
+
+    def start(offset, carry):
+        copy(offset, me).start()
+        return carry
+
+    lax.fori_loop(1, count, start, 0)
+
+    def finish():
+        def wait(offset, carry):
+            copy(offset, lax.rem(me + count - offset, count)).wait()
+            return carry
+
+        own.wait()
+        lax.fori_loop(1, count, wait, 0)
+
+    return finish
 
 
 def segment_kernel(
@@ -130,8 +180,21 @@
 
 
 def pull_kernel(
-    chunk, disp_ref, mass_ref, nodes_ref, part_ref, scale_ref, stiff_ref, pull_ref, ratio_ref, table_ref
+    chunk,
+    disp_ref,
+    mass_ref,
+    nodes_ref,
+    part_ref,
+    scale_ref,
+    stiff_ref,
+    out_ref,
+    pull_ref,
+    ratio_ref,
+    got_ref,
+    table_ref,
+    *semaphores,
 ):
+    finish = exchange(out_ref, got_ref, *semaphores)
     depth = table_ref.shape[0] // 4
     elems = nodes_ref.shape[1]
     parts = stiff_ref.shape[0]
@@ -168,9 +231,11 @@
         0, elems // chunk, one_chunk, jnp.full((1, chunk), jnp.inf, F32)
     )
     ratio_ref[...] = jnp.broadcast_to(jnp.min(best, 1, keepdims=True), ratio_ref.shape)
-
-
-def force_kernel(chunk, pull_ref, nodes_ref, after_ref, force_ref):
+    finish()
+
+
+def force_kernel(chunk, pull_ref, nodes_ref, out_ref, force_ref, got_ref, *semaphores):
+    finish = exchange(out_ref, got_ref, *semaphores)
     depth = force_ref.shape[0] // 3
     force_ref[...] = jnp.zeros_like(force_ref)
 
@@ -186,6 +251,7 @@
         return carry
 
     lax.fori_loop(0, nodes_ref.shape[1] // chunk, one_chunk, 0)
+    finish()
 
 
 def pair_kernel(
@@ -511,7 +577,6 @@
     pair_slot,
     pair_mask,
 ):
-    axes = ("grp", "dev")
     peers, cap = send_blk.shape[1:]
     nodes = node_mass.shape[0]
     blocks, width = seg_node.shape
@@ -532,20 +597,26 @@
         compiler_params=PARAMS,
         name="segments",
     )(ref_pos, displacement, seg_node, seg_mask, send)
-    arrived = lax.all_to_all(outgoing, axes, split_axis=0, concat_axis=0, tiled=True)
 
     chunk = math.gcd(elems, 1024)
     work = 2 * 4 * elems * WIDE * depth
-    pull, ratio = pl.pallas_call(
+    semaphores = [
+        pltpu.SemaphoreType.DMA((peers,)),
+        pltpu.SemaphoreType.DMA((peers,)),
+        pltpu.SemaphoreType.DMA,
+    ]
+    pull, ratio, arrived = pl.pallas_call(
         functools.partial(pull_kernel, chunk),
-        out_shape=(shape(12, elems), shape(8, width)),
-        in_specs=[VMEM, VMEM, VMEM, VMEM, VMEM, SMEM],
-        out_specs=(VMEM, VMEM),
-        scratch_shapes=[pltpu.VMEM((4 * depth, WIDE), F32)],
-        compiler_params=PARAMS,
+        out_shape=(shape(12, elems), shape(8, width), shape(peers, slab, width)),
+        in_specs=[VMEM, VMEM, VMEM, VMEM, VMEM, SMEM, VMEM],
+        out_specs=(VMEM, VMEM, VMEM),
+        scratch_shapes=[pltpu.VMEM((4 * depth, WIDE), F32)] + semaphores,
+        compiler_params=pltpu.CompilerParams(
+            vmem_limit_bytes=LIMIT, collective_id=1, has_side_effects=True
+        ),
         cost_estimate=pl.CostEstimate(flops=12 * work, bytes_accessed=2**20, transcendentals=0),
         name="pulls",
-    )(displacement, mass, elem_nodes, elem_part.reshape(1, -1), elem_scale.reshape(1, -1), part_stiff)
+    )(displacement, mass, elem_nodes, elem_part.reshape(1, -1), elem_scale.reshape(1, -1), part_stiff, outgoing)
 
     group = math.gcd(pairs, 64)
     seg_force, going_back = pl.pallas_call(
@@ -567,17 +638,19 @@
         compiler_params=PARAMS,
         name="pairs",
     )(own, arrived, ratio, pair_a, pair_slot, pair_mask)
-    returned = lax.all_to_all(going_back, axes, split_axis=0, concat_axis=0, tiled=True)
-
-    force = pl.pallas_call(
+
+    force, returned = pl.pallas_call(
         functools.partial(force_kernel, chunk),
-        out_shape=shape(3 * depth, WIDE),
-        in_specs=[VMEM, VMEM, pl.BlockSpec(memory_space=pl.ANY)],
-        out_specs=VMEM,
-        compiler_params=PARAMS,
+        out_shape=(shape(3 * depth, WIDE), shape(peers, slab, width)),
+        in_specs=[VMEM, VMEM, VMEM],
+        out_specs=(VMEM, VMEM),
+        scratch_shapes=semaphores,
+        compiler_params=pltpu.CompilerParams(
+            vmem_limit_bytes=LIMIT, collective_id=2, has_side_effects=True
+        ),
         cost_estimate=pl.CostEstimate(flops=12 * work, bytes_accessed=2**20, transcendentals=0),
         name="forces",
-    )(pull, elem_nodes, seg_force)
+    )(pull, elem_nodes, going_back)
 
     piece = math.gcd(share, 2048)
     total, lower, upper, time_step = pl.pallas_call(

time: 83.4 us -> 79.3 us (0.951)
  starting transfers between devices: 13.1 us -> 0 us
  Pallas kernels: 62 us -> 74.6 us
  waiting for transfers between devices: 2.07 us -> 0 us
  local copies, waits for them, and re-layouts: 5.12 us -> 3.72 us
    all_to_all x2 -> x0, starting transfers between devices: 13.1 us -> none  [the longest x1 7.3 us: shards(): lax.all_to_all(outgoing, axes, split_axis=0, concat_axis=0, tiled=True)]
    pallas_call x1, Pallas kernels: 11.4 us -> 19.7 us  [shards(): pl.pallas_call(functools.partial(pull_kernel, chunk), out_shape=(shape(12...]
    pallas_call x1, Pallas kernels: 8.58 us -> 13.1 us  [shards(): pl.pallas_call(functools.partial(force_kernel, chunk), out_shape=(shape(3...]
    all_to_all x2 -> x0, waiting for transfers between devices: 2.07 us -> none  [the longest x1 2.07 us: shards(): lax.all_to_all(going_back, axes, split_axis=0, concat_axis=0, tiled=True)]
    unnamed x9 -> x7, local copies, waits for them, and re-layouts: 4.44 us -> 3.04 us
  transfers between devices with their start and end apart: 2 -> 0, of which waited for: 1 -> 0; matrix products, arithmetic and copies ran while one was open for 0% -> 0% of each run, Pallas kernels for 24% -> 0%
where the time goes in v7:
time: 79.3 us; the launch traced here: 79 us
  Pallas kernels  74.6 us (94%)
  local copies, waits for them, and re-layouts  3.72 us (5%)
    pallas_call x1, Pallas kernels, shards(): pl.pallas_call(functools.partial(pair_kernel, cap, group), out_shape=(sha...  25.1 us
    pallas_call x1, Pallas kernels, shards(): pl.pallas_call(functools.partial(pull_kernel, chunk), out_shape=(shape(12...  19.7 us
    pallas_call x1, Pallas kernels, shards(): pl.pallas_call(functools.partial(force_kernel, chunk), out_shape=(shape(3...  13.1 us
    pallas_call x1, Pallas kernels, shards(): pl.pallas_call(functools.partial(update_kernel, piece), out_shape=(shape(...  6.84 us
    pallas_call x1, Pallas kernels, shards(): pl.pallas_call(functools.partial(total_kernel, cap, piece), out_shape=(sh...  5.52 us
    pallas_call x1, Pallas kernels, shards(): pl.pallas_call(functools.partial(segment_kernel, cap), out_shape=(shape(b...  4.3 us
    unnamed x7, local copies, waits for them, and re-layouts  3.04 us

profile of v7, /device:TPU:0, one launch (start us, length us, event | category | flops | bytes accessed | tf_op | source)
XLA Modules:
  0.0 79.0 jit_solution(2262445456246248277)
XLA Ops:
  0.6 0.0 copy-start.1
  0.6 0.7 copy-done.1
  1.3 0.1 copy.17
  1.4 0.7 reshape.19.send_ref
  2.1 4.3 %segments.1 = (f32[64,8,128]{2,1,0:T(8,128)}, f32[32,16,128]{2,1,0:T(8,128)}) custom-call(f32[3,8192]{1,0:T(4,128)} %pos_ref.1, f32[3,8192]{1,0:T(4,128)} %disp_ref.5, s32[64,128]{1,0:T(8,128)} %seg_ref.3, s32[64,128]{1,0:T(8,128)} %mask_ref.1, s32[160]{0:T(256)} %reshape.19.send_ref), custom_call_target="tpu_custom_call" | custom-call | tf_op jit(solution)/shard_map/segments/pallas_call | solution.py:591
  6.4 19.7 %pulls.1 = (f32[12,8192]{1,0:T(8,128)}, f32[8,128]{1,0:T(8,128)}, f32[32,16,128]{2,1,0:T(8,128)}) custom-call(f32[3,8192]{1,0:T(4,128)} %disp_ref.5, f32[1,8192]{1,0:T(1,128)} %bitcast.3, s32[4,8192]{1,0:T(4,128)} %nodes_ref.3, s32[1,8192]{1,0:T(1,128)} %bitcast.5, f32[1,8192]{1,0:T(1,128)} %bitcast.6, f32[4]{0:T(128)} %stiff_ref.1, ...), custom_call_target="tpu_custom_call" | custom-call | flops 6442450944 | bytes 1048576 | tf_op jit(solution)/shard_map/pulls/pallas_call | solution.py:608
  26.1 25.1 %pairs.1 = (f32[64,8,128]{2,1,0:T(8,128)}, f32[32,16,128]{2,1,0:T(8,128)}) custom-call(f32[64,8,128]{2,1,0:T(8,128)} %get-tuple-element.17.own_ref, f32[32,16,128]{2,1,0:T(8,128)} %get-tuple-element.18.got_ref, f32[8,128]{1,0:T(8,128)} %get-tuple-element.19.ratio_ref, s32[512]{0:T(512)} %first_ref.1, s32[512]{0:T(512)} %second_ref.1, s32[512]{0:T(512)} %live_ref.1), custom_call_target="tpu_custom_call" | custom-call | tf_op jit(solution)/shard_map/pairs/pallas_call | solution.py:622
  51.3 13.1 %forces.1 = (f32[96,256]{1,0:T(8,128)}, f32[32,16,128]{2,1,0:T(8,128)}) custom-call(f32[12,8192]{1,0:T(8,128)} %get-tuple-element.16.pull_ref, s32[4,8192]{1,0:T(4,128)} %nodes_ref.3, f32[32,16,128]{2,1,0:T(8,128)} %get-tuple-element.20.out_ref), custom_call_target="tpu_custom_call" | custom-call | flops 6442450944 | bytes 1048576 | tf_op jit(solution)/shard_map/forces/pallas_call | solution.py:642
  64.4 5.5 %totals.1 = (f32[96,256]{1,0:T(8,128)}, f32[3,2048]{1,0:T(4,128)}, f32[3,2048]{1,0:T(4,128)}, f32[8,128]{1,0:T(8,128)}) custom-call(f32[32,16,128]{2,1,0:T(8,128)} %get-tuple-element.21.back_ref, s32[160]{0:T(256)} %reshape.19.send_ref, f32[64,8,128]{2,1,0:T(8,128)} %get-tuple-element.22.own_ref, s32[64,128]{1,0:T(8,128)} %seg_ref.3, ...), custom_call_target="tpu_custom_call" | custom-call | tf_op jit(solution)/shard_map/totals/pallas_call | solution.py:656
  69.9 6.8 %update.1 = (f32[3,8192]{1,0:T(4,128)}, f32[3,8192]{1,0:T(4,128)}) custom-call(f32[96,256]{1,0:T(8,128)} %get-tuple-element.24.total_ref, f32[3,2048]{1,0:T(4,128)} %get-tuple-element.25.lower_ref, f32[3,2048]{1,0:T(4,128)} %get-tuple-element.26.upper_ref, s32[2,2048]{1,0:T(2,128)} %shared_ref.3, f32[1,8192]{1,0:T(1,128)} %bitcast.4, f32[3,8192]{1,0:T(4,128)} %vel_ref.1, ...), custom_call_target="tpu_custom_call" | custom-call | tf_op jit(solution)/shard_map/update/pallas_call | solution.py:666
  76.7 0.0 copy-start
  76.7 1.6 %copy.20 = f32[3,8192]{1,0:T(4,128)} copy(f32[3,8192]{1,0:T(4,128)} %get-tuple-element.30) | data formatting | bytes 196608
  78.3 0.0 copy-done
  78.4 0.7 copy.21
Async XLA Ops:
  0.6 0.7 copy-start.1
  76.7 1.6 %copy-start = (f32[3,8192]{1,0:T(4,128)S(1)}, f32[3,8192]{1,0:T(4,128)}, u32[]{:S(2)}) copy-start(f32[3,8192]{1,0:T(4,128)} %get-tuple-element.31) | copy-start | bytes 294916
